TPU v7x, 32 devices: a whole 2x2x4 slice. The times are simulated.
32 devices in a mesh: grp: 2 (over y), wide: 4 (over z), col: 2 (over x), sub: 2 (over core).
Axes of the slice: x: 2, y: 2, z: 4, core: 2. Of those that a mesh axis runs over, the one named last changes fastest.
Arguments:
- inputs: bfloat16 [2048, 28672], P(('grp', 'col', 'sub'), 'wide'), parts along dimension 0, may hold values from -6 to 6
- targets: bfloat16 [2048, 8192], P(('grp', 'wide'), ('col', 'sub')), parts along dimension 0, may hold values from -6 to 6
- weight: bfloat16 [28672, 8192], P('wide', ('col', 'sub')), may hold values from -0.03125 to 0.03125
- factor_in: bfloat16 [16, 28672], P('grp', 'wide'), parts along dimension 0, may hold values from -4 to 4
- factor_out: bfloat16 [16, 8192], P('grp', ('col', 'sub')), parts along dimension 0, may hold values from -4 to 4
Outputs:
- outputs: bfloat16 [2048, 8192], P(('grp', 'wide'), ('col', 'sub')), parts along dimension 0
- weight_step: bfloat16 [57344, 8192], P(('grp', 'wide'), ('col', 'sub')), parts along dimension 0
There are 2 independent parts, one for each index of `grp`. A program takes and returns all parts, laid end to end along the dimension named above; an argument that names none is the same for every part. Nothing has to cross between parts.
All inputs are finite; a program needn't handle non-finite values.
Results may differ from a plain program's by a relative error of at most 0.001.
Values may be sent and summed in bfloat16 or wider, within the bound.
A program may use at most 192 MiB of HBM per device.

v0:
```python
import math

import jax
import jax.numpy as jnp
from jax import lax
from jax.sharding import PartitionSpec as P

D = 8192
FF = 28672
MEMBERS = 8
SEQ = 128


noise_scale = 1.0


def shifted(block, axis, distance):
    devices = range(lax.axis_size(axis))
    route = [((i - distance) % len(devices), i) for i in devices]
    return lax.ppermute(block, axis, route)


def per_device(inputs, targets, weight, factor_in, factor_out):
    gathered = lax.all_gather(inputs, ("col", "sub"), axis=0, tiled=True)
    total_rows = gathered.shape[0]
    cycle_size = lax.axis_size("wide")
    local_rows = total_rows // cycle_size
    my_index = lax.axis_index("wide")
    shaped = gathered.reshape(MEMBERS, SEQ, gathered.shape[1])
    projected = jnp.einsum(
        "msf,mf->ms", shaped, factor_in, preferred_element_type=jnp.float32
    ).reshape(total_rows)
    expanded = jnp.repeat(factor_out, SEQ, axis=0)
    factor_scale = noise_scale / math.sqrt(FF)

    def term_fn(first_row, row_count):
        block = lax.dynamic_slice_in_dim(gathered, first_row, row_count, 0)
        proj_part = lax.dynamic_slice_in_dim(projected, first_row, row_count, 0)
        outer_part = lax.dynamic_slice_in_dim(expanded, first_row, row_count, 0).astype(jnp.float32)
        product = jnp.dot(block, weight, preferred_element_type=jnp.float32)
        return product + factor_scale * proj_part[:, None] * outer_part

    def block_start(step_num):
        which = (my_index - step_num - 1 + 2 * cycle_size) % cycle_size
        return which * local_rows

    running = term_fn(block_start(jnp.int32(0)), local_rows)

    def advance(step_num, carried):
        moved = shifted(carried, "wide", 1)
        return moved + term_fn(block_start(step_num), local_rows)

    perturbed = lax.fori_loop(1, cycle_size, advance, running)
    outputs = perturbed.astype(jnp.bfloat16)
    errors = perturbed - targets.astype(jnp.float32)
    row_sums = jnp.sum(errors * errors, axis=1)
    row_index = my_index * local_rows + jnp.arange(local_rows, dtype=jnp.int32)
    member_of = row_index // SEQ
    onehot = (member_of[:, None] == jnp.arange(MEMBERS, dtype=jnp.int32)[None, :]).astype(
        jnp.float32
    )
    partial_loss = jnp.sum(onehot * row_sums[:, None], axis=0)
    loss = lax.psum(partial_loss, ("wide", "col", "sub")) / (SEQ * D)
    fitness = jnp.mean(loss) - loss
    scaled = factor_in.astype(jnp.float32) * fitness[:, None]
    weight_step = (
        jnp.dot(scaled.T, factor_out.astype(jnp.float32), precision=lax.Precision.HIGHEST)
        / noise_scale
    )
    return (outputs, weight_step.astype(jnp.bfloat16))


def solution(mesh):
    placed = (
        P(("grp", "col", "sub"), "wide"),
        P(("grp", "wide"), ("col", "sub")),
        P("wide", ("col", "sub")),
        P("grp", "wide"),
        P("grp", ("col", "sub")),
    )
    return jax.shard_map(
        per_device,
        mesh=mesh,
        in_specs=placed,
        out_specs=(P(("grp", "wide"), ("col", "sub")), P(("grp", "wide"), ("col", "sub"))),
        check_vma=False,
    )
```

profile of v0, /device:TPU:0, one launch (start us, length us, event | category | flops | bytes accessed | tf_op | source)
XLA Modules:
  0.0 388.7 jit_solution(5863869530332954810)
XLA Ops:
  7.2 0.0 copy-start.2
  7.2 0.0 all-gather.2.cloned.1.call-start
  7.2 0.7 all-gather.2.cloned.1.call-update
  7.9 98.4 %all-gather.2.cloned.1.call-done = bf16[1024,7168]{1,0:T(8,128)(2,1)} async-done(((bf16[256,7168]{1,0:T(8,128)(2,1)}), bf16[1024,7168]{1,0:T(8,128)(2,1)}) %all-gather.2.cloned.1.call-update) | async-done | bytes 14680080 | tf_op jit(solution)/shard_map/all_gather | solution.py:24
  106.3 0.0 copy-done.2
  106.3 0.0 copy-start.3
  106.3 7.2 %fusion.14 = f32[8,1,128]{2,1,0:T(1,128)S(1)} fusion(bf16[8,128,7168]{2,1,0:T(8,128)(2,1)} %bitcast.13, bf16[8,7168,1]{1,0,2:T(8,128)(2,1)S(1)} %bitcast.16), kind=kOutput, calls=%fused_computation.11 | convolution fusion | flops 14680064 | bytes 14798848 | tf_op jit(solution)/shard_map/msf,mf->ms/dot_general | solution.py:30
  113.5 0.1 dynamic-slice_multiply_fusion.1
  113.6 0.0 copy-done.3
  113.6 0.5 broadcast_in_dim.5
  114.1 0.0 copy-start
  114.1 15.9 %fusion.11 = f32[256,2048]{1,0:T(8,128)S(1)} fusion(bf16[7168,2048]{1,0:T(8,128)(2,1)} %param.9, bf16[1024,7168]{1,0:T(8,128)(2,1)} %all-gather.2.cloned.1.call-done, s32[]{:T(128)S(6)} %select_n.57, bf16[1024,2048]{1,0:T(8,128)(2,1)S(1)} %bitcast.14, f32[256]{0:T(256)S(1)} %dynamic-slice_multiply_fusion.1), kind=kOutput, calls=%fused_computation.9 | convolution fusion | flops 7517765632 | bytes 36177920 | tf_op jit(solution)/shard_map/dot_general | solution.py:40
  130.0 0.0 copy-done
  130.0 0.0 copy-start.1
  130.0 192.3 %while.17 = (s32[]{:T(128)}, f32[256,2048]{1,0:T(8,128)S(1)}, s32[]{:T(128)}, bf16[1024,7168]{1,0:T(8,128)(2,1)}, bf16[7168,2048]{1,0:T(8,128)(2,1)}, /*index=5*...) while((s32[]{:T(128)}, f32[256,2048]{1,0:T(8,128)S(1)}, ...), condition=%wide.region_1.2_spmd, body=%wide.region_0.1_spmd.sunk | while | flops 7518290432 | bytes 46666084 | solution.py:53
  130.0 1.5 collective-permute-start
  131.6 0.1 dynamic-slice_multiply_fusion.3
  131.7 48.1 %collective-permute-done = f32[256,2048]{1,0:T(8,128)} collective-permute-done((f32[256,2048]{1,0:T(8,128)S(1)}, f32[256,2048]{1,0:T(8,128)}, u32[]{:S(2)}, u32[]{:S(2)}) %collective-permute-start) | collective-permute-done | bytes 2097184 | tf_op jit(solution)/shard_map/while/body/eval_jaxpr/ppermute | solution.py:20
  179.8 15.2 %fusion.29 = f32[256,2048]{1,0:T(8,128)S(1)} fusion(f32[256,2048]{1,0:T(8,128)} %collective-permute-done, bf16[7168,2048]{1,0:T(8,128)(2,1)} %get-tuple-element.324, bf16[1024,7168]{1,0:T(8,128)(2,1)} %get-tuple-element.323, s32[]{:T(128)S(6)} %select_n.63, bf16[1024,2048]{1,0:T(8,128)(2,1)} %get-tuple-element.326, ...), kind=kOutput, calls=%fused_computation.3.clone.1 | convolution fusion | flops 7518289920 | bytes 38275072 | tf_op jit(solution)/shard_map/while/body/eval_jaxpr/dot_general | solution.py:40
  195.0 0.1 collective-permute-start
  195.1 0.1 dynamic-slice_multiply_fusion.3
  195.2 48.8 %collective-permute-done = f32[256,2048]{1,0:T(8,128)} collective-permute-done((f32[256,2048]{1,0:T(8,128)S(1)}, f32[256,2048]{1,0:T(8,128)}, u32[]{:S(2)}, u32[]{:S(2)}) %collective-permute-start) | collective-permute-done | bytes 2097184 | tf_op jit(solution)/shard_map/while/body/eval_jaxpr/ppermute | solution.py:20
  243.9 15.2 %fusion.29 = f32[256,2048]{1,0:T(8,128)S(1)} fusion(f32[256,2048]{1,0:T(8,128)} %collective-permute-done, bf16[7168,2048]{1,0:T(8,128)(2,1)} %get-tuple-element.324, bf16[1024,7168]{1,0:T(8,128)(2,1)} %get-tuple-element.323, s32[]{:T(128)S(6)} %select_n.63, bf16[1024,2048]{1,0:T(8,128)(2,1)} %get-tuple-element.326, ...), kind=kOutput, calls=%fused_computation.3.clone.1 | convolution fusion | flops 7518289920 | bytes 38275072 | tf_op jit(solution)/shard_map/while/body/eval_jaxpr/dot_general | solution.py:40
  259.2 0.1 collective-permute-start
  259.3 0.1 dynamic-slice_multiply_fusion.3
  259.3 47.8 %collective-permute-done = f32[256,2048]{1,0:T(8,128)} collective-permute-done((f32[256,2048]{1,0:T(8,128)S(1)}, f32[256,2048]{1,0:T(8,128)}, u32[]{:S(2)}, u32[]{:S(2)}) %collective-permute-start) | collective-permute-done | bytes 2097184 | tf_op jit(solution)/shard_map/while/body/eval_jaxpr/ppermute | solution.py:20
  307.2 15.2 %fusion.29 = f32[256,2048]{1,0:T(8,128)S(1)} fusion(f32[256,2048]{1,0:T(8,128)} %collective-permute-done, bf16[7168,2048]{1,0:T(8,128)(2,1)} %get-tuple-element.324, bf16[1024,7168]{1,0:T(8,128)(2,1)} %get-tuple-element.323, s32[]{:T(128)S(6)} %select_n.63, bf16[1024,2048]{1,0:T(8,128)(2,1)} %get-tuple-element.326, ...), kind=kOutput, calls=%fused_computation.3.clone.1 | convolution fusion | flops 7518289920 | bytes 38275072 | tf_op jit(solution)/shard_map/while/body/eval_jaxpr/dot_general | solution.py:40
  322.4 0.0 copy-done.1
  322.4 1.4 multiply_reduce_fusion
  323.8 0.1 select_reduce_fusion
  323.9 29.7 %psum.7 = f32[8]{0:T(128)S(1)} all-reduce(f32[8]{0:T(128)S(1)} %select_reduce_fusion), channel_id=1, replica_groups=mesh['grp'=2,'wide'=4,'col'=2,'sub'=2] {'wide','col','sub'}, use_global_device_ids=true, to_apply=%region_4.5 | all-reduce | flops 8 | bytes 64 | tf_op jit(solution)/shard_map/psum | solution.py:63
  353.6 0.6 multiply_reduce_fusion.1
  354.8 27.0 %convolution_convert_fusion = bf16[7168,2048]{1,0:T(8,128)(2,1)} fusion(bf16[8,2048]{1,0:T(8,128)(2,1)S(1)} %copy-done.3, bf16[8,7168]{1,0:T(8,128)(2,1)S(1)} %copy-done.2, f32[8]{0:T(128)S(1)} %multiply_subtract_fusion), kind=kOutput, calls=%fused_computation.6 | convolution fusion | flops 1424080896 | bytes 29507616 | tf_op jit(solution)/shard_map/dot_general | solution.py:67
  (2 shorter events, 0.0 us)
Async XLA Ops:
  7.2 99.1 %copy-start.2 = (bf16[8,7168]{1,0:T(8,128)(2,1)S(1)}, bf16[8,7168]{1,0:T(8,128)(2,1)}, u32[]{:S(2)}) copy-start(bf16[8,7168]{1,0:T(8,128)(2,1)} %param.10) | copy-start | bytes 344068
  7.2 99.1 %all-gather.2.cloned.1.call-start = ((), (), s32[]{:S(2)}) async-start(), calls=%async_computation | async-start | bytes 18350080 | tf_op jit(solution)/shard_map/all_gather | solution.py:24
  106.3 7.3 %copy-start.3 = (bf16[8,2048]{1,0:T(8,128)(2,1)S(1)}, bf16[8,2048]{1,0:T(8,128)(2,1)}, u32[]{:S(2)}) copy-start(bf16[8,2048]{1,0:T(8,128)(2,1)} %param.11) | copy-start | bytes 98308
  114.1 15.9 %copy-start = (bf16[8,128,2048]{2,1,0:T(8,128)(2,1)}, bf16[8,128,2048]{2,1,0:T(8,128)(2,1)S(1)}, u32[]{:S(2)}) copy-start(bf16[8,128,2048]{2,1,0:T(8,128)(2,1)S(1)} %broadcast_in_dim.5) | copy-start | bytes 12582916
  130.0 192.4 %copy-start.1 = (bf16[256,2048]{1,0:T(8,128)(2,1)S(1)}, bf16[256,2048]{1,0:T(8,128)(2,1)}, u32[]{:S(2)}) copy-start(bf16[256,2048]{1,0:T(8,128)(2,1)} %param.8) | copy-start | bytes 3145732
  130.0 49.8 %collective-permute-start = (f32[256,2048]{1,0:T(8,128)S(1)}, f32[256,2048]{1,0:T(8,128)}, u32[]{:S(2)}, u32[]{:S(2)}) collective-permute-start(f32[256,2048]{1,0:T(8,128)S(1)} %get-tuple-element.307), channel_id=1, source_target_pairs={{12,0},{0,4},{4,8},{8,12},{13,1},{1,5},{5,9},{9,13},{14,2},{2,6},{... | collective-permute-start | bytes 6291464 | tf_op jit(solution)/shard_map/while/body/eval_jaxpr/ppermute | solution.py:20
  195.0 48.9 %collective-permute-start = (f32[256,2048]{1,0:T(8,128)S(1)}, f32[256,2048]{1,0:T(8,128)}, u32[]{:S(2)}, u32[]{:S(2)}) collective-permute-start(f32[256,2048]{1,0:T(8,128)S(1)} %get-tuple-element.307), channel_id=1, source_target_pairs={{12,0},{0,4},{4,8},{8,12},{13,1},{1,5},{5,9},{9,13},{14,2},{2,6},{... | collective-permute-start | bytes 6291464 | tf_op jit(solution)/shard_map/while/body/eval_jaxpr/ppermute | solution.py:20
  259.2 48.0 %collective-permute-start = (f32[256,2048]{1,0:T(8,128)S(1)}, f32[256,2048]{1,0:T(8,128)}, u32[]{:S(2)}, u32[]{:S(2)}) collective-permute-start(f32[256,2048]{1,0:T(8,128)S(1)} %get-tuple-element.307), channel_id=1, source_target_pairs={{12,0},{0,4},{4,8},{8,12},{13,1},{1,5},{5,9},{9,13},{14,2},{2,6},{... | collective-permute-start | bytes 6291464 | tf_op jit(solution)/shard_map/while/body/eval_jaxpr/ppermute | solution.py:20
Sparse Core Ops, SparseCore 0:
  9.6 96.6 all-gather.1
where the time goes:
time: 389 us
  waiting for transfers between devices  244 us (63%)
  matrix products  95.6 us (25%)
  blocking collectives  29.7 us (8%)
  between operations  14.8 us (4%)
    ppermute x3, waiting for transfers between devices, shifted(): return lax.ppermute(block, axis, route)  145 us
    all_gather x1, waiting for transfers between devices, per_device(): gathered = lax.all_gather(inputs, ('col', 'sub'), axis=0, tiled=True)  98.4 us
    dot_general x4, matrix products, term_fn(): product = jnp.dot(block, weight, preferred_element_type=jnp.float32)  61.5 us
    psum x1, blocking collectives, per_device(): loss = lax.psum(partial_loss, ('wide', 'col', 'sub')) / (SEQ * D)  29.7 us
    dot_general x1, matrix products, per_device(): jnp.dot(scaled.T, factor_out.astype(jnp.float32), precision=lax.Precision...  27 us
  transfers between devices with their start and end apart: 4, of which 4 were waited for; matrix products, arithmetic and copies ran while one was open for 0% of the time, Pallas kernels for 0%

commit v1 on v0

v1 whole, which is shorter than its diff:
```python
import math

import jax
import jax.numpy as jnp
from jax import lax
from jax.sharding import PartitionSpec as P

D = 8192
FF = 28672
MEMBERS = 8
SEQ = 128
PIECES = 4
SPAN = 250.0
FLOOR = -124.0


noise_scale = 1.0


def encode(rows):
    top = jnp.max(jnp.abs(rows), axis=-1, keepdims=True)
    scale = lax.reduce_precision(jnp.maximum(top, 1e-30) * 1.01, 8, 7)
    height = jnp.exp2(jnp.abs(rows) * (SPAN / scale) + FLOOR)
    code = jnp.where(rows < 0, -height, height).astype(jnp.bfloat16)
    side = jnp.broadcast_to(scale, rows.shape[:-1] + (128,)).astype(jnp.bfloat16)
    return jnp.concatenate([code, side], axis=-1)


def decode(message):
    code = message[..., :-128].astype(jnp.float32)
    scale = message[..., -128:-127].astype(jnp.float32)
    size = (jnp.log2(jnp.abs(code)) - FLOOR) * (scale / SPAN)
    return jnp.where(code < 0, -size, size)


def exchanged(block, axis, bit):
    route = [(i, i ^ bit) for i in range(lax.axis_size(axis))]
    return lax.ppermute(block, axis, route)


def piece_product(gathered, weight, factor_in, factor_out, first_row, blocks, height, local_rows):
    members = [(b * local_rows + first_row) // SEQ for b in range(blocks)]
    fi = jnp.stack([factor_in[m] for m in members])
    fo = jnp.stack([factor_out[m] for m in members]).astype(jnp.float32)
    shaped = gathered.reshape(blocks, height, gathered.shape[1])
    projected = jnp.einsum("bhf,bf->bh", shaped, fi, preferred_element_type=jnp.float32)
    product = jnp.dot(gathered, weight, preferred_element_type=jnp.float32)
    product = product.reshape(blocks, height, weight.shape[1])
    factor_scale = noise_scale / math.sqrt(FF)
    return product + factor_scale * projected[:, :, None] * fo[:, None, :]


def reduce_scattered(product, me):
    held = product
    cycle = lax.axis_size("wide")
    bit = 1
    while bit < cycle:
        held = held.reshape((held.shape[0] // 2, 2) + held.shape[1:])
        mine = (me // bit) % 2
        sent = lax.dynamic_index_in_dim(held, 1 - mine, 1, keepdims=False)
        kept = lax.dynamic_index_in_dim(held, mine, 1, keepdims=False)
        held = kept + decode(exchanged(encode(sent), "wide", bit))
        bit *= 2
    return held[0]


def per_device(inputs, targets, weight, factor_in, factor_out):
    cycle = lax.axis_size("wide")
    local_rows = targets.shape[0]
    me = lax.axis_index("wide")
    per_shard = inputs.shape[0] // local_rows
    height = local_rows // PIECES
    shaped = inputs.reshape(per_shard, PIECES, height, inputs.shape[1])

    sums = []
    for j in range(PIECES):
        own = shaped[:, j].reshape(per_shard * height, inputs.shape[1])
        gathered = lax.all_gather(own, ("col", "sub"), axis=0, tiled=True)
        product = piece_product(
            gathered, weight, factor_in, factor_out, j * height, cycle, height, local_rows
        )
        sums.append(reduce_scattered(product, me))
    perturbed = jnp.concatenate(sums, axis=0)
    outputs = perturbed.astype(jnp.bfloat16)
    errors = perturbed - targets.astype(jnp.float32)
    row_sums = jnp.sum(errors * errors, axis=1)
    row_index = me * local_rows + jnp.arange(local_rows, dtype=jnp.int32)
    member_of = row_index // SEQ
    onehot = (member_of[:, None] == jnp.arange(MEMBERS, dtype=jnp.int32)[None, :]).astype(
        jnp.float32
    )
    partial_loss = jnp.sum(onehot * row_sums[:, None], axis=0)
    loss = lax.psum(partial_loss, ("wide", "col", "sub")) / (SEQ * D)
    fitness = jnp.mean(loss) - loss
    side = factor_out.astype(jnp.float32) * fitness[:, None]
    high = lax.reduce_precision(side, 8, 7)
    rest = side - high
    middle = lax.reduce_precision(rest, 8, 7)
    low = rest - middle
    right = jnp.concatenate([high, middle, low], axis=0).astype(jnp.bfloat16)
    left = jnp.concatenate([factor_in] * 3, axis=0)
    weight_step = (
        lax.dot_general(
            left, right, (((0,), (0,)), ((), ())), preferred_element_type=jnp.float32
        )
        / noise_scale
    )
    return (outputs, weight_step.astype(jnp.bfloat16))


def solution(mesh):
    placed = (
        P(("grp", "col", "sub"), "wide"),
        P(("grp", "wide"), ("col", "sub")),
        P("wide", ("col", "sub")),
        P("grp", "wide"),
        P("grp", ("col", "sub")),
    )
    return jax.shard_map(
        per_device,
        mesh=mesh,
        in_specs=placed,
        out_specs=(P(("grp", "wide"), ("col", "sub")), P(("grp", "wide"), ("col", "sub"))),
        check_vma=False,
    )
```

time: 389 us -> 352 us (0.905)
  waiting for transfers between devices: 244 us -> 195 us
  matrix products: 95.6 us -> 83.8 us
  starting transfers between devices: 1.7 us -> 11.4 us
  other arithmetic: 2.43 us -> 11 us
  local copies, waits for them, and re-layouts: 0.55 us -> 4.95 us
    ppermute x3 -> x8, waiting for transfers between devices: 145 us -> 71.5 us  [exchanged(): return lax.ppermute(block, axis, route)]
    all_gather x1 -> x4, waiting for transfers between devices: 98.4 us -> 122 us  [per_device(): gathered = lax.all_gather(own, ('col', 'sub'), axis=0, tiled=True)]
    dot_general x6 -> x9, matrix products: 95.6 us -> 83.8 us  [the longest x4 57 us: piece_product(): product = jnp.dot(gathered, weight, preferred_element_type=jnp.float32)]
    ppermute x3 -> x8, starting transfers between devices: 1.66 us -> 11.2 us  [exchanged(): return lax.ppermute(block, axis, route)]
    slice x0 -> x2, local copies, waits for them, and re-layouts: none -> 4.13 us  [the longest x1 3.94 us: per_device(): own = shaped[:, j].reshape(per_shard * height, inputs.shape[1])]
  transfers between devices with their start and end apart: 4 -> 12, of which waited for: 4 -> 10; matrix products, arithmetic and copies ran while one was open for 0% -> 4% of each run, Pallas kernels for 0% -> 0%
where the time goes in v1:
time: 352 us
  waiting for transfers between devices  195 us (55%)
  matrix products  83.8 us (24%)
  blocking collectives  30.5 us (9%)
  between operations  14.9 us (4%)
  starting transfers between devices  11.4 us (3%)
  other arithmetic  11 us (3%)
  local copies, waits for them, and re-layouts  4.95 us (1%)
    all_gather x4, waiting for transfers between devices, per_device(): gathered = lax.all_gather(own, ('col', 'sub'), axis=0, tiled=True)  122 us
    ppermute x8, waiting for transfers between devices, exchanged(): return lax.ppermute(block, axis, route)  71.5 us
    dot_general x4, matrix products, piece_product(): product = jnp.dot(gathered, weight, preferred_element_type=jnp.float32)  57 us
    psum x1, blocking collectives, per_device(): loss = lax.psum(partial_loss, ('wide', 'col', 'sub')) / (SEQ * D)  30.5 us
    dot_general x1, matrix products, per_device(): lax.dot_general(left, right, (((0,), (0,)), ((), ())), preferred_element_...  14.3 us
    dot_general x4, matrix products, piece_product(): jnp.einsum('bhf,bf->bh', shaped, fi, preferred_element_type=jnp.float32)  12.5 us
    ppermute x8, starting transfers between devices, exchanged(): return lax.ppermute(block, axis, route)  11.2 us
  transfers between devices with their start and end apart: 12, of which 10 were waited for; matrix products, arithmetic and copies ran while one was open for 4% of the time, Pallas kernels for 0%

profile of v1, /device:TPU:0, one launch (start us, length us, event | category | flops | bytes accessed | tf_op | source)
XLA Modules:
  0.0 351.9 jit_solution(17884061261170513131)
XLA Ops:
  7.2 3.9 %fusion.101 = (bf16[1,1,64,7168]{3,2,1,0:T(8,128)(2,1)}, bf16[1,1,64,7168]{3,2,1,0:T(8,128)(2,1)}, bf16[1,1,64,7168]{3,2,1,0:T(8,128)(2,1)}, bf16[1,1,64,7168]{3,2,1,0:T(8,128)(2,1)}) fusion(bf16[1,4,64,7168]{3,2,1,0:T(8,128)(2,1)} %bitcast.129), kind=kLoop, calls=%fused_computation.213 | loop fusion | bytes 7340032 | tf_op jit(solution)/shard_map/slice | solution.py:77
  11.2 0.7 all-gather.11.cloned.1.call-update
  12.0 0.7 all-gather.13.cloned.1.call-update
  12.7 0.5 all-gather.15.cloned.1.call-update
  13.7 0.2 fusion.102
  13.9 0.1 maximum_bitcast_fusion
  14.0 0.1 maximum_bitcast_fusion.1
  14.2 31.4 %all-gather.9.cloned.1.call-done = bf16[1,1,256,7168]{3,2,1,0:T(8,128)(2,1)} async-done(((bf16[1,1,64,7168]{3,2,1,0:T(8,128)(2,1)}), bf16[1,1,256,7168]{3,2,1,0:T(8,128)(2,1)}) %all-gather.9.cloned.1.call-update) | async-done | bytes 3670032 | tf_op jit(solution)/shard_map/all_gather | solution.py:78
  45.5 3.1 fusion.89
  48.6 30.0 %all-gather.11.cloned.1.call-done = bf16[1,1,256,7168]{3,2,1,0:T(8,128)(2,1)} async-done(((bf16[1,1,64,7168]{3,2,1,0:T(8,128)(2,1)}), bf16[1,1,256,7168]{3,2,1,0:T(8,128)(2,1)}) %all-gather.11.cloned.1.call-update) | async-done | bytes 3670032 | tf_op jit(solution)/shard_map/all_gather | solution.py:78
  78.6 3.1 fusion.87
  81.7 30.0 %all-gather.13.cloned.1.call-done = bf16[1,1,256,7168]{3,2,1,0:T(8,128)(2,1)} async-done(((bf16[1,1,64,7168]{3,2,1,0:T(8,128)(2,1)}), bf16[1,1,256,7168]{3,2,1,0:T(8,128)(2,1)}) %all-gather.13.cloned.1.call-update) | async-done | bytes 3670032 | tf_op jit(solution)/shard_map/all_gather | solution.py:78
  111.7 3.1 fusion.85
  114.8 30.5 %all-gather.15.cloned.1.call-done = bf16[1,1,256,7168]{3,2,1,0:T(8,128)(2,1)} async-done(((bf16[1,1,64,7168]{3,2,1,0:T(8,128)(2,1)}), bf16[1,1,256,7168]{3,2,1,0:T(8,128)(2,1)}) %all-gather.15.cloned.1.call-update) | async-done | bytes 3670032 | tf_op jit(solution)/shard_map/all_gather | solution.py:78
  145.3 3.2 fusion.83
  148.6 13.6 %fusion.2 = f32[256,2048]{1,0:T(8,128)S(1)} fusion(bf16[7168,2048]{1,0:T(8,128)(2,1)} %param.7, bf16[1,1,256,7168]{3,2,1,0:T(8,128)(2,1)S(1)} %copy-done.3), kind=kOutput, calls=%fused_computation.3 | convolution fusion | flops 7516192768 | bytes 35127296 | tf_op jit(solution)/shard_map/dot_general | solution.py:47
  162.2 14.4 %fusion = f32[256,2048]{1,0:T(8,128)S(1)} fusion(bf16[7168,2048]{1,0:T(8,128)(2,1)} %param.7, bf16[1,1,256,7168]{3,2,1,0:T(8,128)(2,1)} %all-gather.15.cloned.1.call-done), kind=kOutput, calls=%fused_computation.1 | convolution fusion | flops 7516192768 | bytes 35127296 | tf_op jit(solution)/shard_map/dot_general | solution.py:47
  176.6 0.4 copy_add_fusion.1
  177.0 0.2 abs_reduce_fusion.1
  177.2 0.2 abs_reduce_fusion
  177.3 14.4 %fusion.4 = f32[256,2048]{1,0:T(8,128)S(1)} fusion(bf16[7168,2048]{1,0:T(8,128)(2,1)} %param.7, bf16[1,1,256,7168]{3,2,1,0:T(8,128)(2,1)} %all-gather.11.cloned.1.call-done), kind=kOutput, calls=%fused_computation.5 | convolution fusion | flops 7516192768 | bytes 35127296 | tf_op jit(solution)/shard_map/dot_general | solution.py:47
  191.7 14.6 %fusion.6 = f32[256,2048]{1,0:T(8,128)S(1)} fusion(bf16[7168,2048]{1,0:T(8,128)(2,1)} %param.7, bf16[1,1,256,7168]{3,2,1,0:T(8,128)(2,1)} %all-gather.9.cloned.1.call-done), kind=kOutput, calls=%fused_computation.7 | convolution fusion | flops 7516192768 | bytes 35127296 | tf_op jit(solution)/shard_map/dot_general | solution.py:47
  206.3 0.4 copy_add_fusion.3
  206.7 0.2 abs_reduce_fusion.3
  206.9 0.2 abs_reduce_fusion.2
  207.1 0.4 fusion.27
  207.5 0.4 fusion.25
  207.9 0.4 fusion.31
  208.3 0.4 fusion.29
  208.8 1.6 collective-permute-start.4
  210.5 0.6 collective-permute-start.6
  211.3 1.6 collective-permute-start
  213.0 0.6 collective-permute-start.2
  213.6 10.8 %collective-permute-done.4 = bf16[2,64,2176]{2,1,0:T(8,128)(2,1)S(1)} collective-permute-done((bf16[2,64,2176]{2,1,0:T(8,128)(2,1)S(1)}, bf16[2,64,2176]{2,1,0:T(8,128)(2,1)S(1)}, u32[]{:S(2)}, u32[]{:S(2)}) %collective-permute-start.4) | collective-permute-done | bytes 557088 | tf_op jit(solution)/shard_map/ppermute | solution.py:38
  224.5 0.4 fusion.30
  224.9 0.1 abs_reduce_fusion.5
  225.0 0.2 fusion.67
  225.4 2.5 collective-permute-start.5
  227.9 14.4 %collective-permute-done.6 = bf16[2,64,2176]{2,1,0:T(8,128)(2,1)S(1)} collective-permute-done((bf16[2,64,2176]{2,1,0:T(8,128)(2,1)S(1)}, bf16[2,64,2176]{2,1,0:T(8,128)(2,1)S(1)}, u32[]{:S(2)}, u32[]{:S(2)}) %collective-permute-start.6) | collective-permute-done | bytes 557088 | tf_op jit(solution)/shard_map/ppermute | solution.py:38
  242.4 0.4 fusion.32
  242.8 0.1 abs_reduce_fusion.4
  242.9 0.2 fusion.70
  243.3 1.5 collective-permute-start.7
  244.8 15.4 %collective-permute-done = bf16[2,64,2176]{2,1,0:T(8,128)(2,1)S(1)} collective-permute-done((bf16[2,64,2176]{2,1,0:T(8,128)(2,1)S(1)}, bf16[2,64,2176]{2,1,0:T(8,128)(2,1)S(1)}, u32[]{:S(2)}, u32[]{:S(2)}) %collective-permute-start) | collective-permute-done | bytes 557088 | tf_op jit(solution)/shard_map/ppermute | solution.py:38
  260.3 0.4 fusion.26
  260.7 0.1 abs_reduce_fusion.7
  260.8 0.2 fusion.61
  261.2 1.5 collective-permute-start.1
  262.7 8.8 %collective-permute-done.2 = bf16[2,64,2176]{2,1,0:T(8,128)(2,1)S(1)} collective-permute-done((bf16[2,64,2176]{2,1,0:T(8,128)(2,1)S(1)}, bf16[2,64,2176]{2,1,0:T(8,128)(2,1)S(1)}, u32[]{:S(2)}, u32[]{:S(2)}) %collective-permute-start.2) | collective-permute-done | bytes 557088 | tf_op jit(solution)/shard_map/ppermute | solution.py:38
  271.6 0.4 fusion.28
  272.0 0.1 abs_reduce_fusion.6
  272.2 0.2 fusion.64
  272.6 1.5 collective-permute-start.3
  274.3 0.2 fusion.69
  274.5 0.2 fusion.72
  274.7 16.5 %collective-permute-done.1 = bf16[1,64,2176]{2,1,0:T(8,128)(2,1)S(1)} collective-permute-done((bf16[1,64,2176]{2,1,0:T(8,128)(2,1)S(1)}, bf16[1,64,2176]{2,1,0:T(8,128)(2,1)S(1)}, u32[]{:S(2)}, u32[]{:S(2)}) %collective-permute-start.1) | collective-permute-done | bytes 278560 | tf_op jit(solution)/shard_map/ppermute | solution.py:38
  291.4 0.2 fusion.63
  291.6 5.5 %collective-permute-done.3 = bf16[1,64,2176]{2,1,0:T(8,128)(2,1)S(1)} collective-permute-done((bf16[1,64,2176]{2,1,0:T(8,128)(2,1)S(1)}, bf16[1,64,2176]{2,1,0:T(8,128)(2,1)S(1)}, u32[]{:S(2)}, u32[]{:S(2)}) %collective-permute-start.3) | collective-permute-done | bytes 278560 | tf_op jit(solution)/shard_map/ppermute | solution.py:38
  297.3 0.2 fusion.66
  297.5 0.4 multiply_reduce_fusion
  298.0 1.1 fusion.8
  299.1 30.5 %psum.7 = f32[8]{0:T(128)S(1)} all-reduce(f32[8]{0:T(128)S(1)} %select_reduce_fusion), channel_id=1, replica_groups=mesh['grp'=2,'wide'=4,'col'=2,'sub'=2] {'wide','col','sub'}, use_global_device_ids=true, to_apply=%region_10.11 | all-reduce | flops 8 | bytes 64 | tf_op jit(solution)/shard_map/psum | solution.py:93
  329.6 0.6 multiply_reduce_fusion.9
  331.0 14.3 %convolution_convert_fusion = bf16[7168,2048]{1,0:T(8,128)(2,1)} fusion(bf16[8,7168]{1,0:T(8,128)(2,1)S(1)} %copy-done.1, bf16[8,2048]{1,0:T(8,128)(2,1)S(1)} %get-tuple-element.15, bf16[8,2048]{1,0:T(8,128)(2,1)S(1)} %get-tuple-element.16, bf16[8,2048]{1,0:T(8,128)(2,1)S(1)} %get-tuple-element.14), kind=kOutput, calls=%fused_computation | convolution fusion | flops 720650240 | bytes 29573120 | tf_op jit(solution)/shard_map/dot_general | solution.py:103
  (65 shorter events, 2.5 us)
Async XLA Ops:
  7.2 38.4 %all-gather.9.cloned.1.call-start = ((), (), s32[]{:S(2)}) async-start(), calls=%async_computation | async-start | bytes 4587520 | tf_op jit(solution)/shard_map/all_gather | solution.py:78
  11.1 2.1 copy-start.2
  11.1 2.5 copy-start.1
  11.2 67.5 %all-gather.11.cloned.1.call-start = ((), (), s32[]{:S(2)}) async-start(), calls=%async_computation.1 | async-start | bytes 4587520 | tf_op jit(solution)/shard_map/all_gather | solution.py:78
  11.9 99.8 %all-gather.13.cloned.1.call-start = ((), (), s32[]{:S(2)}) async-start(), calls=%async_computation.2 | async-start | bytes 4587520 | tf_op jit(solution)/shard_map/all_gather | solution.py:78
  12.7 132.6 %all-gather.15.cloned.1.call-start = ((), (), s32[]{:S(2)}) async-start(), calls=%async_computation.3 | async-start | bytes 4587520 | tf_op jit(solution)/shard_map/all_gather | solution.py:78
  145.3 3.3 copy-start.3
  208.8 15.5 %collective-permute-start.4 = (bf16[2,64,2176]{2,1,0:T(8,128)(2,1)S(1)}, bf16[2,64,2176]{2,1,0:T(8,128)(2,1)S(1)}, u32[]{:S(2)}, u32[]{:S(2)}) collective-permute-start(bf16[2,64,2176]{2,1,0:T(8,128)(2,1)S(1)} %pad_maximum_fusion.3), channel_id=1, source_target_pairs={{0,4},{4,0},{8,12},{12,8},{1,5},{5,1},{9,13},{13,9},{2,6},{6,2},{1... | collective-permute-start | bytes 1671176 | tf_op jit(solution)/shard_map/ppermute | solution.py:38
  210.5 31.7 %collective-permute-start.6 = (bf16[2,64,2176]{2,1,0:T(8,128)(2,1)S(1)}, bf16[2,64,2176]{2,1,0:T(8,128)(2,1)S(1)}, u32[]{:S(2)}, u32[]{:S(2)}) collective-permute-start(bf16[2,64,2176]{2,1,0:T(8,128)(2,1)S(1)} %pad_maximum_fusion.4), channel_id=1, source_target_pairs={{0,4},{4,0},{8,12},{12,8},{1,5},{5,1},{9,13},{13,9},{2,6},{6,2},{1... | collective-permute-start | bytes 1671176 | tf_op jit(solution)/shard_map/ppermute | solution.py:38
  211.3 48.9 %collective-permute-start = (bf16[2,64,2176]{2,1,0:T(8,128)(2,1)S(1)}, bf16[2,64,2176]{2,1,0:T(8,128)(2,1)S(1)}, u32[]{:S(2)}, u32[]{:S(2)}) collective-permute-start(bf16[2,64,2176]{2,1,0:T(8,128)(2,1)S(1)} %pad_maximum_fusion.1), channel_id=1, source_target_pairs={{0,4},{4,0},{8,12},{12,8},{1,5},{5,1},{9,13},{13,9},{2,6},{6,2},{1... | collective-permute-start | bytes 1671176 | tf_op jit(solution)/shard_map/ppermute | solution.py:38
  213.0 58.6 %collective-permute-start.2 = (bf16[2,64,2176]{2,1,0:T(8,128)(2,1)S(1)}, bf16[2,64,2176]{2,1,0:T(8,128)(2,1)S(1)}, u32[]{:S(2)}, u32[]{:S(2)}) collective-permute-start(bf16[2,64,2176]{2,1,0:T(8,128)(2,1)S(1)} %pad_maximum_fusion.2), channel_id=1, source_target_pairs={{0,4},{4,0},{8,12},{12,8},{1,5},{5,1},{9,13},{13,9},{2,6},{6,2},{1... | collective-permute-start | bytes 1671176 | tf_op jit(solution)/shard_map/ppermute | solution.py:38
  225.4 48.6 %collective-permute-start.5 = (bf16[1,64,2176]{2,1,0:T(8,128)(2,1)S(1)}, bf16[1,64,2176]{2,1,0:T(8,128)(2,1)S(1)}, u32[]{:S(2)}, u32[]{:S(2)}) collective-permute-start(bf16[1,64,2176]{2,1,0:T(8,128)(2,1)S(1)} %pad_maximum_fusion.7), channel_id=1, source_target_pairs={{0,8},{4,12},{8,0},{12,4},{1,9},{5,13},{9,1},{13,5},{2,10},{6,14},... | collective-permute-start | bytes 835592 | tf_op jit(solution)/shard_map/ppermute | solution.py:38
  243.3 30.9 %collective-permute-start.7 = (bf16[1,64,2176]{2,1,0:T(8,128)(2,1)S(1)}, bf16[1,64,2176]{2,1,0:T(8,128)(2,1)S(1)}, u32[]{:S(2)}, u32[]{:S(2)}) collective-permute-start(bf16[1,64,2176]{2,1,0:T(8,128)(2,1)S(1)} %pad_maximum_fusion.8), channel_id=1, source_target_pairs={{0,8},{4,12},{8,0},{12,4},{1,9},{5,13},{9,1},{13,5},{2,10},{6,14},... | collective-permute-start | bytes 835592 | tf_op jit(solution)/shard_map/ppermute | solution.py:38
  261.2 30.1 %collective-permute-start.1 = (bf16[1,64,2176]{2,1,0:T(8,128)(2,1)S(1)}, bf16[1,64,2176]{2,1,0:T(8,128)(2,1)S(1)}, u32[]{:S(2)}, u32[]{:S(2)}) collective-permute-start(bf16[1,64,2176]{2,1,0:T(8,128)(2,1)S(1)} %pad_maximum_fusion.5), channel_id=1, source_target_pairs={{0,8},{4,12},{8,0},{12,4},{1,9},{5,13},{9,1},{13,5},{2,10},{6,14},... | collective-permute-start | bytes 835592 | tf_op jit(solution)/shard_map/ppermute | solution.py:38
  272.6 24.6 %collective-permute-start.3 = (bf16[1,64,2176]{2,1,0:T(8,128)(2,1)S(1)}, bf16[1,64,2176]{2,1,0:T(8,128)(2,1)S(1)}, u32[]{:S(2)}, u32[]{:S(2)}) collective-permute-start(bf16[1,64,2176]{2,1,0:T(8,128)(2,1)S(1)} %pad_maximum_fusion.6), channel_id=1, source_target_pairs={{0,8},{4,12},{8,0},{12,4},{1,9},{5,13},{9,1},{13,5},{2,10},{6,14},... | collective-permute-start | bytes 835592 | tf_op jit(solution)/shard_map/ppermute | solution.py:38
  274.5 23.0 %copy-start = (bf16[256,2048]{1,0:T(8,128)(2,1)S(1)}, bf16[256,2048]{1,0:T(8,128)(2,1)}, u32[]{:S(2)}) copy-start(bf16[256,2048]{1,0:T(8,128)(2,1)} %param.6) | copy-start | bytes 3145732
Sparse Core Ops, SparseCore 0:
  11.3 34.1 all-gather.8
  47.1 31.4 all-gather.10
  80.2 31.4 all-gather.12
  113.7 31.4 all-gather.14

commit v2 on v1

--- a/solution.py
+++ b/solution.py
@@ -38,48 +38,77 @@
     return lax.ppermute(block, axis, route)
 
 
-def piece_product(gathered, weight, factor_in, factor_out, first_row, blocks, height, local_rows):
-    members = [(b * local_rows + first_row) // SEQ for b in range(blocks)]
-    fi = jnp.stack([factor_in[m] for m in members])
-    fo = jnp.stack([factor_out[m] for m in members]).astype(jnp.float32)
-    shaped = gathered.reshape(blocks, height, gathered.shape[1])
+def bits_of(size):
+    return [1 << k for k in range(size.bit_length() - 1)]
+
+
+def spread(block):
+    held = [block]
+    for axis in ("col", "sub"):
+        for bit in reversed(bits_of(lax.axis_size(axis))):
+            held = [part for b in held for part in (b, exchanged(b, axis, bit))]
+    return held
+
+
+def piece_product(rows, weight, factor_in, factor_out, members, height):
+    blocks = rows.shape[0] // height
+    fi = jnp.take(factor_in, members, axis=0)
+    fo = jnp.take(factor_out, members, axis=0).astype(jnp.float32)
+    shaped = rows.reshape(blocks, height, rows.shape[1])
     projected = jnp.einsum("bhf,bf->bh", shaped, fi, preferred_element_type=jnp.float32)
-    product = jnp.dot(gathered, weight, preferred_element_type=jnp.float32)
+    product = jnp.dot(rows, weight, preferred_element_type=jnp.float32)
     product = product.reshape(blocks, height, weight.shape[1])
     factor_scale = noise_scale / math.sqrt(FF)
     return product + factor_scale * projected[:, :, None] * fo[:, None, :]
 
 
-def reduce_scattered(product, me):
-    held = product
-    cycle = lax.axis_size("wide")
-    bit = 1
-    while bit < cycle:
-        held = held.reshape((held.shape[0] // 2, 2) + held.shape[1:])
-        mine = (me // bit) % 2
-        sent = lax.dynamic_index_in_dim(held, 1 - mine, 1, keepdims=False)
-        kept = lax.dynamic_index_in_dim(held, mine, 1, keepdims=False)
-        held = kept + decode(exchanged(encode(sent), "wide", bit))
-        bit *= 2
-    return held[0]
+def halves(held, bit, me, flip):
+    held = held.reshape((held.shape[0] // 2, 2) + held.shape[1:])
+    mine = ((me // bit) % 2) ^ ((flip // bit) % 2)
+    sent = lax.dynamic_index_in_dim(held, 1 - mine, 1, keepdims=False)
+    kept = lax.dynamic_index_in_dim(held, mine, 1, keepdims=False)
+    return encode(sent), kept
 
 
 def per_device(inputs, targets, weight, factor_in, factor_out):
     cycle = lax.axis_size("wide")
     local_rows = targets.shape[0]
     me = lax.axis_index("wide")
+    shard = lax.axis_index("col") * lax.axis_size("sub") + lax.axis_index("sub")
     per_shard = inputs.shape[0] // local_rows
     height = local_rows // PIECES
     shaped = inputs.reshape(per_shard, PIECES, height, inputs.shape[1])
+    flip = shard * per_shard
+    order = jnp.arange(cycle, dtype=jnp.int32) ^ flip
 
-    sums = []
-    for j in range(PIECES):
-        own = shaped[:, j].reshape(per_shard * height, inputs.shape[1])
-        gathered = lax.all_gather(own, ("col", "sub"), axis=0, tiled=True)
-        product = piece_product(
-            gathered, weight, factor_in, factor_out, j * height, cycle, height, local_rows
-        )
-        sums.append(reduce_scattered(product, me))
+    parts = [
+        spread(shaped[:, j].reshape(per_shard * height, inputs.shape[1])) for j in range(PIECES)
+    ]
+    stages = bits_of(cycle)
+    held = [None] * PIECES
+    pending = [None] * PIECES
+    after = []
+    for turn in range(PIECES + len(stages)):
+        made = []
+        if turn < PIECES:
+            ready, _ = lax.optimization_barrier((parts[turn], after))
+            members = (order * local_rows + turn * height) // SEQ
+            product = piece_product(
+                jnp.concatenate(ready, axis=0), weight, factor_in, factor_out, members, height
+            )
+            pending[turn] = halves(product, stages[0], me, flip)
+            made.append(pending[turn][0])
+        for j in range(min(turn, PIECES)):
+            stage = turn - j - 1
+            if stage >= len(stages):
+                continue
+            message, kept = pending[j]
+            held[j] = kept + decode(exchanged(message, "wide", stages[stage]))
+            if stage + 1 < len(stages):
+                pending[j] = halves(held[j], stages[stage + 1], me, flip)
+                made.append(pending[j][0])
+        after = made
+    sums = [h[0] for h in held]
     perturbed = jnp.concatenate(sums, axis=0)
     outputs = perturbed.astype(jnp.bfloat16)
     errors = perturbed - targets.astype(jnp.float32)
@@ -90,7 +119,10 @@
         jnp.float32
     )
     partial_loss = jnp.sum(onehot * row_sums[:, None], axis=0)
-    loss = lax.psum(partial_loss, ("wide", "col", "sub")) / (SEQ * D)
+    for axis in ("sub", "col", "wide"):
+        for bit in bits_of(lax.axis_size(axis)):
+            partial_loss = partial_loss + exchanged(partial_loss, axis, bit)
+    loss = partial_loss / (SEQ * D)
     fitness = jnp.mean(loss) - loss
     side = factor_out.astype(jnp.float32) * fitness[:, None]
     high = lax.reduce_precision(side, 8, 7)

time: 352 us -> 249 us (0.71)
  waiting for transfers between devices: 195 us -> 105 us
  blocking collectives: 30.5 us -> 0 us
  local copies, waits for them, and re-layouts: 4.95 us -> 27.9 us
  between operations: 14.9 us -> 1.94 us
  starting transfers between devices: 11.4 us -> 20.7 us
    all_gather x4 -> x0, waiting for transfers between devices: 122 us -> none  [per_device(): gathered = lax.all_gather(own, ('col', 'sub'), axis=0, tiled=True)]
    ppermute x8 -> x24, waiting for transfers between devices: 71.5 us -> 105 us  [exchanged(): return lax.ppermute(block, axis, route)]
    psum x1 -> x0, blocking collectives: 30.5 us -> none  [per_device(): loss = lax.psum(partial_loss, ('wide', 'col', 'sub')) / (SEQ * D)]
    unnamed x8 -> x18, local copies, waits for them, and re-layouts: 0.02 us -> 16.1 us
    ppermute x8 -> x24, starting transfers between devices: 11.2 us -> 20.7 us  [exchanged(): return lax.ppermute(block, axis, route)]
    gather x0 -> x8, local copies, waits for them, and re-layouts: none -> 4.71 us  [the longest x4 2.41 us: piece_product(): fi = jnp.take(factor_in, members, axis=0)]
    slice x2 -> x0, local copies, waits for them, and re-layouts: 4.13 us -> none  [the longest x1 3.94 us: per_device(): own = shaped[:, j].reshape(per_shard * height, inputs.shape[1])]
  transfers between devices with their start and end apart: 12 -> 24, of which waited for: 10 -> 9; matrix products, arithmetic and copies ran while one was open for 4% -> 41% of each run, Pallas kernels for 0% -> 0%
where the time goes in v2:
time: 249 us; the launch traced here: 248 us
  waiting for transfers between devices  105 us (42%)
  matrix products  81.4 us (33%)
  local copies, waits for them, and re-layouts  27.9 us (11%)
  starting transfers between devices  20.7 us (8%)
  other arithmetic  11.8 us (5%)
    ppermute x24, waiting for transfers between devices, exchanged(): return lax.ppermute(block, axis, route)  105 us
    dot_general x4, matrix products, piece_product(): product = jnp.dot(rows, weight, preferred_element_type=jnp.float32)  56.8 us
    ppermute x24, starting transfers between devices, exchanged(): return lax.ppermute(block, axis, route)  20.7 us
    unnamed x18, local copies, waits for them, and re-layouts  16.1 us
    dot_general x1, matrix products, per_device(): lax.dot_general(left, right, (((0,), (0,)), ((), ())), preferred_element_...  14.3 us
    dot_general x4, matrix products, piece_product(): jnp.einsum('bhf,bf->bh', shaped, fi, preferred_element_type=jnp.float32)  10.3 us
  transfers between devices with their start and end apart: 24, of which 9 were waited for; matrix products, arithmetic and copies ran while one was open for 41% of the time, Pallas kernels for 0%

profile of v2, /device:TPU:0, one launch (start us, length us, event | category | flops | bytes accessed | tf_op | source)
XLA Modules:
  0.0 248.4 jit_solution(17369302702129069686)
XLA Ops:
  0.6 3.2 %slice_bitcast_fusion.3 = (bf16[64,7168]{1,0:T(8,128)(2,1)}, bf16[64,7168]{1,0:T(8,128)(2,1)S(1)}, bf16[64,7168]{1,0:T(8,128)(2,1)S(1)}, bf16[64,7168]{1,0:T(8,128)(2,1)S(1)}) fusion(bf16[1,4,64,7168]{3,2,1,0:T(8,128)(2,1)} %bitcast.113), kind=kLoop, calls=%fused_computation.79 | loop fusion | bytes 7340032 | tf_op jit(solution)/shard_map/reshape;squeeze | solution.py:85
  3.9 2.9 %collective-permute-start.1 = (bf16[64,7168]{1,0:T(8,128)(2,1)}, bf16[64,7168]{1,0:T(8,128)(2,1)}, u32[]{:S(2)}, u32[]{:S(2)}) collective-permute-start(bf16[64,7168]{1,0:T(8,128)(2,1)} %get-tuple-element.20), channel_id=1, source_target_pairs={{0,2},{2,0},{1,3},{3,1},{4,6},{6,4},{5,7},{7,5},{8,10},{10,8},{9,1... | collective-permute-start | bytes 2752520 | tf_op jit(solution)/shard_map/ppermute | solution.py:38
  6.9 0.4 collective-permute-start.15
  7.3 1.7 collective-permute-start.6
  9.2 0.6 gather_fusion.7
  9.7 0.6 gather_fusion.3
  10.3 0.6 gather_fusion.2
  10.9 0.6 gather_fusion.6
  11.6 0.6 gather_fusion.1
  12.1 0.6 gather_fusion
  12.8 0.6 gather_fusion.5
  13.3 0.6 gather_fusion.4
  14.9 13.4 %collective-permute-done.1 = bf16[64,7168]{1,0:T(8,128)(2,1)} collective-permute-done((bf16[64,7168]{1,0:T(8,128)(2,1)}, bf16[64,7168]{1,0:T(8,128)(2,1)}, u32[]{:S(2)}, u32[]{:S(2)}) %collective-permute-start.1) | collective-permute-done | bytes 917536 | tf_op jit(solution)/shard_map/ppermute | solution.py:38
  28.4 0.6 collective-permute-start.5
  29.0 37.8 %collective-permute-done.6 = bf16[64,7168]{1,0:T(8,128)(2,1)} collective-permute-done((bf16[64,7168]{1,0:T(8,128)(2,1)S(1)}, bf16[64,7168]{1,0:T(8,128)(2,1)}, u32[]{:S(2)}, u32[]{:S(2)}) %collective-permute-start.6) | collective-permute-done | bytes 917536 | tf_op jit(solution)/shard_map/ppermute | solution.py:38
  66.8 1.7 collective-permute-start.11
  68.5 1.2 constant_dynamic-update-slice_fusion.3
  69.8 1.2 constant_dynamic-update-slice_fusion.2
  71.0 1.2 constant_dynamic-update-slice_fusion.1
  72.3 1.0 fusion.76
  73.4 13.4 %fusion.94 = f32[256,2048]{1,0:T(8,128)S(1)} fusion(bf16[256,7168]{1,0:T(8,128)(2,1)S(1)} %constant_dynamic-update-slice_fusion, bf16[7168,2048]{1,0:T(8,128)(2,1)} %param.11), kind=kOutput, calls=%fused_computation.259 | convolution fusion | flops 7516192768 | bytes 35127296 | tf_op jit(solution)/shard_map/dot_general | solution.py:59
  87.3 0.4 fusion.17
  87.8 0.6 collective-permute-start.10
  88.5 0.4 collective-permute-start.12
  88.9 1.6 collective-permute-start.3
  90.5 1.0 constant_dynamic-update-slice_fusion.7
  91.5 1.0 constant_dynamic-update-slice_fusion.6
  92.4 2.2 constant_dynamic-update-slice_fusion.5
  94.6 1.0 constant_dynamic-update-slice_fusion.4
  95.6 14.4 %fusion.95 = f32[256,2048]{1,0:T(8,128)S(1)} fusion(bf16[256,7168]{1,0:T(8,128)(2,1)} %constant_dynamic-update-slice_fusion.4, bf16[7168,2048]{1,0:T(8,128)(2,1)} %param.11), kind=kOutput, calls=%fused_computation.260 | convolution fusion | flops 7516192768 | bytes 35127296 | tf_op jit(solution)/shard_map/dot_general | solution.py:59
  110.0 3.1 %fusion.74 = f32[4,1,64]{2,1,0:T(1,128)S(1)} fusion(bf16[4,64,7168]{2,1,0:T(8,128)(2,1)} %bitcast.14, bf16[4,7168,1]{1,0,2:T(4,128)(2,1)S(1)} %select_bitcast_fusion.2), kind=kOutput, calls=%fused_computation.145 | convolution fusion | flops 3670016 | bytes 3728384 | tf_op jit(solution)/shard_map/bhf,bf->bh/dot_general | solution.py:58
  114.1 0.5 collective-permute-start.8
  114.7 0.4 fusion.18
  115.6 2.7 %collective-permute-start.4 = (bf16[1,64,2176]{2,1,0:T(8,128)(2,1)S(1)}, bf16[1,64,2176]{2,1,0:T(8,128)(2,1)S(1)}, u32[]{:S(2)}, u32[]{:S(2)}) collective-permute-start(bf16[1,64,2176]{2,1,0:T(8,128)(2,1)S(1)} %pad_maximum_fusion.5), channel_id=1, source_target_pairs={{0,8},{4,12},{8,0},{12,4},{1,9},{5,13},{9,1},{13,5},{2,10},{6,14},... | collective-permute-start | bytes 835592 | tf_op jit(solution)/shard_map/ppermute | solution.py:38
  118.3 16.2 %collective-permute-done.8 = bf16[2,64,2176]{2,1,0:T(8,128)(2,1)S(1)} collective-permute-done((bf16[2,64,2176]{2,1,0:T(8,128)(2,1)S(1)}, bf16[2,64,2176]{2,1,0:T(8,128)(2,1)S(1)}, u32[]{:S(2)}, u32[]{:S(2)}) %collective-permute-start.8) | collective-permute-done | bytes 557088 | tf_op jit(solution)/shard_map/ppermute | solution.py:38
  134.6 0.4 fusion.20
  135.5 0.6 collective-permute-start.9
  136.1 1.0 constant_dynamic-update-slice_fusion.11
  137.1 1.0 constant_dynamic-update-slice_fusion.10
  138.1 1.0 constant_dynamic-update-slice_fusion.9
  139.0 1.0 constant_dynamic-update-slice_fusion.8
  140.0 14.4 %fusion.96 = f32[256,2048]{1,0:T(8,128)S(1)} fusion(bf16[256,7168]{1,0:T(8,128)(2,1)} %constant_dynamic-update-slice_fusion.8, bf16[7168,2048]{1,0:T(8,128)(2,1)} %param.11), kind=kOutput, calls=%fused_computation.261 | convolution fusion | flops 7516192768 | bytes 35127296 | tf_op jit(solution)/shard_map/dot_general | solution.py:59
  154.4 3.1 %fusion.72 = f32[4,1,64]{2,1,0:T(1,128)S(1)} fusion(bf16[4,64,7168]{2,1,0:T(8,128)(2,1)} %bitcast.25, bf16[4,7168,1]{1,0,2:T(4,128)(2,1)S(1)} %select_bitcast_fusion.1), kind=kOutput, calls=%fused_computation.143 | convolution fusion | flops 3670016 | bytes 3728384 | tf_op jit(solution)/shard_map/bhf,bf->bh/dot_general | solution.py:58
  158.5 2.5 %collective-permute-start.13 = (bf16[2,64,2176]{2,1,0:T(8,128)(2,1)S(1)}, bf16[2,64,2176]{2,1,0:T(8,128)(2,1)S(1)}, u32[]{:S(2)}, u32[]{:S(2)}) collective-permute-start(bf16[2,64,2176]{2,1,0:T(8,128)(2,1)S(1)} %pad_maximum_fusion.3), channel_id=1, source_target_pairs={{0,4},{4,0},{8,12},{12,8},{1,5},{5,1},{9,13},{13,9},{2,6},{6,2},{1... | collective-permute-start | bytes 1671176 | tf_op jit(solution)/shard_map/ppermute | solution.py:38
  161.1 1.0 constant_dynamic-update-slice_fusion.15
  162.0 2.2 constant_dynamic-update-slice_fusion.14
  164.2 2.2 constant_dynamic-update-slice_fusion.13
  166.4 1.0 constant_dynamic-update-slice_fusion.12
  167.3 14.6 %fusion.97 = f32[256,2048]{1,0:T(8,128)S(1)} fusion(bf16[256,7168]{1,0:T(8,128)(2,1)} %constant_dynamic-update-slice_fusion.12, bf16[7168,2048]{1,0:T(8,128)(2,1)} %param.11), kind=kOutput, calls=%fused_computation.262 | convolution fusion | flops 7516192768 | bytes 35127296 | tf_op jit(solution)/shard_map/dot_general | solution.py:59
  182.0 3.1 %fusion.70 = f32[4,1,64]{2,1,0:T(1,128)S(1)} fusion(bf16[4,64,7168]{2,1,0:T(8,128)(2,1)} %bitcast.36, bf16[4,7168,1]{1,0,2:T(4,128)(2,1)S(1)} %select_bitcast_fusion), kind=kOutput, calls=%fused_computation.141 | convolution fusion | flops 3670016 | bytes 3728384 | tf_op jit(solution)/shard_map/bhf,bf->bh/dot_general | solution.py:58
  187.0 0.4 fusion.22
  187.9 1.9 collective-permute-start.14
  189.8 15.2 %collective-permute-done.18 = bf16[2,64,2176]{2,1,0:T(8,128)(2,1)S(1)} collective-permute-done((bf16[2,64,2176]{2,1,0:T(8,128)(2,1)S(1)}, bf16[2,64,2176]{2,1,0:T(8,128)(2,1)S(1)}, u32[]{:S(2)}, u32[]{:S(2)}) %collective-permute-start.18) | collective-permute-done | bytes 557088 | tf_op jit(solution)/shard_map/ppermute | solution.py:38
  205.1 0.4 fusion.24
  206.5 11.5 %collective-permute-done.19 = bf16[1,64,2176]{2,1,0:T(8,128)(2,1)S(1)} collective-permute-done((bf16[1,64,2176]{2,1,0:T(8,128)(2,1)S(1)}, bf16[1,64,2176]{2,1,0:T(8,128)(2,1)S(1)}, u32[]{:S(2)}, u32[]{:S(2)}) %collective-permute-start.19) | collective-permute-done | bytes 278560 | tf_op jit(solution)/shard_map/ppermute | solution.py:38
  218.3 1.2 fusion
  220.0 1.1 collective-permute-done.20
  221.2 1.3 collective-permute-start.21
  222.5 2.2 collective-permute-done.21
  224.7 3.5 %collective-permute-done.22 = f32[8]{0:T(128)S(1)} collective-permute-done((f32[8]{0:T(128)S(1)}, f32[8]{0:T(128)S(1)}, u32[]{:S(2)}, u32[]{:S(2)}) %collective-permute-start.22) | collective-permute-done | bytes 64 | tf_op jit(solution)/shard_map/ppermute | solution.py:38
  228.2 0.7 collective-permute-start.23
  229.0 3.7 %collective-permute-done.23 = f32[8]{0:T(128)S(1)} collective-permute-done((f32[8]{0:T(128)S(1)}, f32[8]{0:T(128)S(1)}, u32[]{:S(2)}, u32[]{:S(2)}) %collective-permute-start.23) | collective-permute-done | bytes 64 | tf_op jit(solution)/shard_map/ppermute | solution.py:38
  232.7 0.6 fusion.93
  234.0 14.3 %convolution_convert_fusion = bf16[7168,2048]{1,0:T(8,128)(2,1)} fusion(bf16[8,7168]{1,0:T(8,128)(2,1)S(1)} %copy-done, bf16[8,2048]{1,0:T(8,128)(2,1)S(1)} %get-tuple-element.41, bf16[8,2048]{1,0:T(8,128)(2,1)S(1)} %get-tuple-element.42, bf16[8,2048]{1,0:T(8,128)(2,1)S(1)} %get-tuple-element.40), kind=kOutput, calls=%fused_computation.8 | convolution fusion | flops 720650240 | bytes 29573120 | tf_op jit(solution)/shard_map/dot_general | solution.py:135
  (126 shorter events, 9.3 us)
Async XLA Ops:
  0.6 8.5 %copy-start.1 = (bf16[8,2048]{1,0:T(8,128)(2,1)S(1)}, bf16[8,2048]{1,0:T(8,128)(2,1)}, u32[]{:S(2)}) copy-start(bf16[8,2048]{1,0:T(8,128)(2,1)} %param.13) | copy-start | bytes 98308
  0.6 9.7 %copy-start = (bf16[8,7168]{1,0:T(8,128)(2,1)S(1)}, bf16[8,7168]{1,0:T(8,128)(2,1)}, u32[]{:S(2)}) copy-start(bf16[8,7168]{1,0:T(8,128)(2,1)} %param.12) | copy-start | bytes 344068
  3.9 24.4 %collective-permute-start.1 = (bf16[64,7168]{1,0:T(8,128)(2,1)}, bf16[64,7168]{1,0:T(8,128)(2,1)}, u32[]{:S(2)}, u32[]{:S(2)}) collective-permute-start(bf16[64,7168]{1,0:T(8,128)(2,1)} %get-tuple-element.20), channel_id=1, source_target_pairs={{0,2},{2,0},{1,3},{3,1},{4,6},{6,4},{5,7},{7,5},{8,10},{10,8},{9,1... | collective-permute-start | bytes 2752520 | tf_op jit(solution)/shard_map/ppermute | solution.py:38
  6.8 21.6 %collective-permute-start = (bf16[64,7168]{1,0:T(8,128)(2,1)}, bf16[64,7168]{1,0:T(8,128)(2,1)}, u32[]{:S(2)}, u32[]{:S(2)}) collective-permute-start(bf16[64,7168]{1,0:T(8,128)(2,1)} %get-tuple-element.20), channel_id=1, source_target_pairs={{0,1},{1,0},{2,3},{3,2},{4,5},{5,4},{6,7},{7,6},{8,9},{9,8},{10,11... | collective-permute-start | bytes 2752520 | tf_op jit(solution)/shard_map/ppermute | solution.py:38
  6.8 81.0 %collective-permute-start.16 = (bf16[64,7168]{1,0:T(8,128)(2,1)S(1)}, bf16[64,7168]{1,0:T(8,128)(2,1)}, u32[]{:S(2)}, u32[]{:S(2)}) collective-permute-start(bf16[64,7168]{1,0:T(8,128)(2,1)S(1)} %get-tuple-element.32), channel_id=1, source_target_pairs={{0,2},{2,0},{1,3},{3,1},{4,6},{6,4},{5,7},{7,5},{8,10},{10,8},{9,1... | collective-permute-start | bytes 2752520 | tf_op jit(solution)/shard_map/ppermute | solution.py:38
  6.9 154.2 %collective-permute-start.15 = (bf16[64,7168]{1,0:T(8,128)(2,1)S(1)}, bf16[64,7168]{1,0:T(8,128)(2,1)}, u32[]{:S(2)}, u32[]{:S(2)}) collective-permute-start(bf16[64,7168]{1,0:T(8,128)(2,1)S(1)} %get-tuple-element.32), channel_id=1, source_target_pairs={{0,1},{1,0},{2,3},{3,2},{4,5},{5,4},{6,7},{7,6},{8,9},{9,8},{10,11... | collective-permute-start | bytes 2752520 | tf_op jit(solution)/shard_map/ppermute | solution.py:38
  7.3 59.5 %collective-permute-start.6 = (bf16[64,7168]{1,0:T(8,128)(2,1)S(1)}, bf16[64,7168]{1,0:T(8,128)(2,1)}, u32[]{:S(2)}, u32[]{:S(2)}) collective-permute-start(bf16[64,7168]{1,0:T(8,128)(2,1)S(1)} %get-tuple-element.24), channel_id=1, source_target_pairs={{0,2},{2,0},{1,3},{3,1},{4,6},{6,4},{5,7},{7,5},{8,10},{10,8},{9,1... | collective-permute-start | bytes 2752520 | tf_op jit(solution)/shard_map/ppermute | solution.py:38
  28.3 40.2 %collective-permute-start.2 = (bf16[64,7168]{1,0:T(8,128)(2,1)}, bf16[64,7168]{1,0:T(8,128)(2,1)S(1)}, u32[]{:S(2)}, u32[]{:S(2)}) collective-permute-start(bf16[64,7168]{1,0:T(8,128)(2,1)} %collective-permute-done.1), channel_id=1, source_target_pairs={{0,1},{1,0},{2,3},{3,2},{4,5},{5,4},{6,7},{7,6},{8,9},{9,8},{10,11... | collective-permute-start | bytes 2752520 | tf_op jit(solution)/shard_map/ppermute | solution.py:38
  28.4 60.1 %collective-permute-start.5 = (bf16[64,7168]{1,0:T(8,128)(2,1)S(1)}, bf16[64,7168]{1,0:T(8,128)(2,1)S(1)}, u32[]{:S(2)}, u32[]{:S(2)}) collective-permute-start(bf16[64,7168]{1,0:T(8,128)(2,1)S(1)} %get-tuple-element.24), channel_id=1, source_target_pairs={{0,1},{1,0},{2,3},{3,2},{4,5},{5,4},{6,7},{7,6},{8,9},{9,8},{10,11... | collective-permute-start | bytes 2752520 | tf_op jit(solution)/shard_map/ppermute | solution.py:38
  66.8 21.6 %collective-permute-start.11 = (bf16[64,7168]{1,0:T(8,128)(2,1)S(1)}, bf16[64,7168]{1,0:T(8,128)(2,1)S(1)}, u32[]{:S(2)}, u32[]{:S(2)}) collective-permute-start(bf16[64,7168]{1,0:T(8,128)(2,1)S(1)} %get-tuple-element.28), channel_id=1, source_target_pairs={{0,2},{2,0},{1,3},{3,1},{4,6},{6,4},{5,7},{7,5},{8,10},{10,8},{9,1... | collective-permute-start | bytes 2752520 | tf_op jit(solution)/shard_map/ppermute | solution.py:38
  68.5 20.4 %collective-permute-start.7 = (bf16[64,7168]{1,0:T(8,128)(2,1)}, bf16[64,7168]{1,0:T(8,128)(2,1)S(1)}, u32[]{:S(2)}, u32[]{:S(2)}) collective-permute-start(bf16[64,7168]{1,0:T(8,128)(2,1)} %collective-permute-done.6), channel_id=1, source_target_pairs={{0,1},{1,0},{2,3},{3,2},{4,5},{5,4},{6,7},{7,6},{8,9},{9,8},{10,11... | collective-permute-start | bytes 2752520 | tf_op jit(solution)/shard_map/ppermute | solution.py:38
  87.8 27.8 %collective-permute-start.10 = (bf16[64,7168]{1,0:T(8,128)(2,1)S(1)}, bf16[64,7168]{1,0:T(8,128)(2,1)S(1)}, u32[]{:S(2)}, u32[]{:S(2)}) collective-permute-start(bf16[64,7168]{1,0:T(8,128)(2,1)S(1)} %get-tuple-element.28), channel_id=1, source_target_pairs={{0,1},{1,0},{2,3},{3,2},{4,5},{5,4},{6,7},{7,6},{8,9},{9,8},{10,11... | collective-permute-start | bytes 2752520 | tf_op jit(solution)/shard_map/ppermute | solution.py:38
  88.4 72.7 %collective-permute-start.17 = (bf16[64,7168]{1,0:T(8,128)(2,1)}, bf16[64,7168]{1,0:T(8,128)(2,1)S(1)}, u32[]{:S(2)}, u32[]{:S(2)}) collective-permute-start(bf16[64,7168]{1,0:T(8,128)(2,1)} %collective-permute-done.16), channel_id=1, source_target_pairs={{0,1},{1,0},{2,3},{3,2},{4,5},{5,4},{6,7},{7,6},{8,9},{9,8},{10,11... | collective-permute-start | bytes 2752520 | tf_op jit(solution)/shard_map/ppermute | solution.py:38
  88.5 29.8 %collective-permute-start.12 = (bf16[64,7168]{1,0:T(8,128)(2,1)S(1)}, bf16[64,7168]{1,0:T(8,128)(2,1)S(1)}, u32[]{:S(2)}, u32[]{:S(2)}) collective-permute-start(bf16[64,7168]{1,0:T(8,128)(2,1)S(1)} %collective-permute-done.11), channel_id=1, source_target_pairs={{0,1},{1,0},{2,3},{3,2},{4,5},{5,4},{6,7},{7,6},{8,9},{9,8},{10,11... | collective-permute-start | bytes 2752520 | tf_op jit(solution)/shard_map/ppermute | solution.py:38
  88.9 25.2 %collective-permute-start.3 = (bf16[2,64,2176]{2,1,0:T(8,128)(2,1)S(1)}, bf16[2,64,2176]{2,1,0:T(8,128)(2,1)S(1)}, u32[]{:S(2)}, u32[]{:S(2)}) collective-permute-start(bf16[2,64,2176]{2,1,0:T(8,128)(2,1)S(1)} %pad_maximum_fusion.1), channel_id=1, source_target_pairs={{0,4},{4,0},{8,12},{12,8},{1,5},{5,1},{9,13},{13,9},{2,6},{6,2},{1... | collective-permute-start | bytes 1671176 | tf_op jit(solution)/shard_map/ppermute | solution.py:38
  114.1 20.4 %collective-permute-start.8 = (bf16[2,64,2176]{2,1,0:T(8,128)(2,1)S(1)}, bf16[2,64,2176]{2,1,0:T(8,128)(2,1)S(1)}, u32[]{:S(2)}, u32[]{:S(2)}) collective-permute-start(bf16[2,64,2176]{2,1,0:T(8,128)(2,1)S(1)} %pad_maximum_fusion.2), channel_id=1, source_target_pairs={{0,4},{4,0},{8,12},{12,8},{1,5},{5,1},{9,13},{13,9},{2,6},{6,2},{1... | collective-permute-start | bytes 1671176 | tf_op jit(solution)/shard_map/ppermute | solution.py:38
  115.6 70.5 %collective-permute-start.4 = (bf16[1,64,2176]{2,1,0:T(8,128)(2,1)S(1)}, bf16[1,64,2176]{2,1,0:T(8,128)(2,1)S(1)}, u32[]{:S(2)}, u32[]{:S(2)}) collective-permute-start(bf16[1,64,2176]{2,1,0:T(8,128)(2,1)S(1)} %pad_maximum_fusion.5), channel_id=1, source_target_pairs={{0,8},{4,12},{8,0},{12,4},{1,9},{5,13},{9,1},{13,5},{2,10},{6,14},... | collective-permute-start | bytes 835592 | tf_op jit(solution)/shard_map/ppermute | solution.py:38
  135.5 51.0 %collective-permute-start.9 = (bf16[1,64,2176]{2,1,0:T(8,128)(2,1)S(1)}, bf16[1,64,2176]{2,1,0:T(8,128)(2,1)S(1)}, u32[]{:S(2)}, u32[]{:S(2)}) collective-permute-start(bf16[1,64,2176]{2,1,0:T(8,128)(2,1)S(1)} %pad_maximum_fusion.6), channel_id=1, source_target_pairs={{0,8},{4,12},{8,0},{12,4},{1,9},{5,13},{9,1},{13,5},{2,10},{6,14},... | collective-permute-start | bytes 835592 | tf_op jit(solution)/shard_map/ppermute | solution.py:38
  158.5 28.4 %collective-permute-start.13 = (bf16[2,64,2176]{2,1,0:T(8,128)(2,1)S(1)}, bf16[2,64,2176]{2,1,0:T(8,128)(2,1)S(1)}, u32[]{:S(2)}, u32[]{:S(2)}) collective-permute-start(bf16[2,64,2176]{2,1,0:T(8,128)(2,1)S(1)} %pad_maximum_fusion.3), channel_id=1, source_target_pairs={{0,4},{4,0},{8,12},{12,8},{1,5},{5,1},{9,13},{13,9},{2,6},{6,2},{1... | collective-permute-start | bytes 1671176 | tf_op jit(solution)/shard_map/ppermute | solution.py:38
  186.1 18.9 %collective-permute-start.18 = (bf16[2,64,2176]{2,1,0:T(8,128)(2,1)S(1)}, bf16[2,64,2176]{2,1,0:T(8,128)(2,1)S(1)}, u32[]{:S(2)}, u32[]{:S(2)}) collective-permute-start(bf16[2,64,2176]{2,1,0:T(8,128)(2,1)S(1)} %pad_maximum_fusion.4), channel_id=1, source_target_pairs={{0,4},{4,0},{8,12},{12,8},{1,5},{5,1},{9,13},{13,9},{2,6},{6,2},{1... | collective-permute-start | bytes 1671176 | tf_op jit(solution)/shard_map/ppermute | solution.py:38
  187.9 18.2 %collective-permute-start.14 = (bf16[1,64,2176]{2,1,0:T(8,128)(2,1)S(1)}, bf16[1,64,2176]{2,1,0:T(8,128)(2,1)S(1)}, u32[]{:S(2)}, u32[]{:S(2)}) collective-permute-start(bf16[1,64,2176]{2,1,0:T(8,128)(2,1)S(1)} %pad_maximum_fusion.7), channel_id=1, source_target_pairs={{0,8},{4,12},{8,0},{12,4},{1,9},{5,13},{9,1},{13,5},{2,10},{6,14},... | collective-permute-start | bytes 835592 | tf_op jit(solution)/shard_map/ppermute | solution.py:38
  205.7 13.8 %copy-start.2 = (bf16[256,2048]{1,0:T(8,128)(2,1)S(1)}, bf16[256,2048]{1,0:T(8,128)(2,1)}, u32[]{:S(2)}) copy-start(bf16[256,2048]{1,0:T(8,128)(2,1)} %param.10) | copy-start | bytes 3145732
  206.0 11.9 %collective-permute-start.19 = (bf16[1,64,2176]{2,1,0:T(8,128)(2,1)S(1)}, bf16[1,64,2176]{2,1,0:T(8,128)(2,1)S(1)}, u32[]{:S(2)}, u32[]{:S(2)}) collective-permute-start(bf16[1,64,2176]{2,1,0:T(8,128)(2,1)S(1)} %pad_maximum_fusion.8), channel_id=1, source_target_pairs={{0,8},{4,12},{8,0},{12,4},{1,9},{5,13},{9,1},{13,5},{2,10},{6,14},... | collective-permute-start | bytes 835592 | tf_op jit(solution)/shard_map/ppermute | solution.py:38
  220.0 1.2 collective-permute-start.20
  221.2 3.5 %collective-permute-start.21 = (f32[8]{0:T(128)S(1)}, f32[8]{0:T(128)S(1)}, u32[]{:S(2)}, u32[]{:S(2)}) collective-permute-start(f32[8]{0:T(128)S(1)} %add.212), channel_id=1, source_target_pairs={{0,2},{2,0},{1,3},{3,1},{4,6},{6,4},{5,7},{7,5},{8,10},{10,8},{9,1... | collective-permute-start | bytes 104 | tf_op jit(solution)/shard_map/ppermute | solution.py:38
  224.7 3.5 %collective-permute-start.22 = (f32[8]{0:T(128)S(1)}, f32[8]{0:T(128)S(1)}, u32[]{:S(2)}, u32[]{:S(2)}) collective-permute-start(f32[8]{0:T(128)S(1)} %add.213), channel_id=1, source_target_pairs={{0,4},{4,0},{8,12},{12,8},{1,5},{5,1},{9,13},{13,9},{2,6},{6,2},{1... | collective-permute-start | bytes 104 | tf_op jit(solution)/shard_map/ppermute | solution.py:38
  228.2 4.4 %collective-permute-start.23 = (f32[8]{0:T(128)S(1)}, f32[8]{0:T(128)S(1)}, u32[]{:S(2)}, u32[]{:S(2)}) collective-permute-start(f32[8]{0:T(128)S(1)} %add.214), channel_id=1, source_target_pairs={{0,8},{4,12},{8,0},{12,4},{1,9},{5,13},{9,1},{13,5},{2,10},{6,14},... | collective-permute-start | bytes 104 | tf_op jit(solution)/shard_map/ppermute | solution.py:38

commit v3 on v2

--- a/solution.py
+++ b/solution.py
@@ -9,7 +9,7 @@
 FF = 28672
 MEMBERS = 8
 SEQ = 128
-PIECES = 4
+SHARES = (2, 2, 2, 2)
 SPAN = 250.0
 FLOOR = -124.0
 
@@ -42,24 +42,20 @@
     return [1 << k for k in range(size.bit_length() - 1)]
 
 
-def spread(block):
-    held = [block]
-    for axis in ("col", "sub"):
-        for bit in reversed(bits_of(lax.axis_size(axis))):
-            held = [part for b in held for part in (b, exchanged(b, axis, bit))]
+def crossed(block, axis):
+    held = block if isinstance(block, list) else [block]
+    for bit in reversed(bits_of(lax.axis_size(axis))):
+        held = [part for b in held for part in (b, exchanged(b, axis, bit))]
     return held
 
 
-def piece_product(rows, weight, factor_in, factor_out, members, height):
-    blocks = rows.shape[0] // height
-    fi = jnp.take(factor_in, members, axis=0)
-    fo = jnp.take(factor_out, members, axis=0).astype(jnp.float32)
-    shaped = rows.reshape(blocks, height, rows.shape[1])
-    projected = jnp.einsum("bhf,bf->bh", shaped, fi, preferred_element_type=jnp.float32)
+def piece_product(rows, weight, projected, fo):
+    blocks, units, height = projected.shape
     product = jnp.dot(rows, weight, preferred_element_type=jnp.float32)
-    product = product.reshape(blocks, height, weight.shape[1])
+    product = product.reshape(blocks, units, height, weight.shape[1])
     factor_scale = noise_scale / math.sqrt(FF)
-    return product + factor_scale * projected[:, :, None] * fo[:, None, :]
+    product = product + factor_scale * projected[..., None] * fo[:, :, None, :]
+    return product.reshape(blocks, units * height, weight.shape[1])
 
 
 def halves(held, bit, me, flip):
@@ -76,29 +72,53 @@
     me = lax.axis_index("wide")
     shard = lax.axis_index("col") * lax.axis_size("sub") + lax.axis_index("sub")
     per_shard = inputs.shape[0] // local_rows
-    height = local_rows // PIECES
-    shaped = inputs.reshape(per_shard, PIECES, height, inputs.shape[1])
+    total_units = sum(SHARES)
+    height = local_rows // total_units
+    units = jnp.arange(total_units, dtype=jnp.int32) * height
     flip = shard * per_shard
     order = jnp.arange(cycle, dtype=jnp.int32) ^ flip
 
-    parts = [
-        spread(shaped[:, j].reshape(per_shard * height, inputs.shape[1])) for j in range(PIECES)
-    ]
+    own_blocks = flip + jnp.arange(per_shard, dtype=jnp.int32)
+    own_members = (own_blocks[:, None] * local_rows + units[None, :]) // SEQ
+    own_projected = jnp.einsum(
+        "buhf,buf->buh",
+        inputs.reshape(per_shard, total_units, height, inputs.shape[1]),
+        jnp.take(factor_in, own_members, axis=0),
+        preferred_element_type=jnp.float32,
+    )
+    projected = jnp.concatenate(crossed(crossed(own_projected, "col"), "sub"), axis=0)
+    members = (order[:, None] * local_rows + units[None, :]) // SEQ
+    expanded = jnp.take(factor_out, members, axis=0).astype(jnp.float32)
+
+    shaped = inputs.reshape(per_shard, local_rows, inputs.shape[1])
+    firsts = [sum(SHARES[:j]) for j in range(len(SHARES))]
+    parts, arrived = [], []
+    for first, share in zip(firsts, SHARES):
+        own = shaped[:, first * height : (first + share) * height].reshape(-1, inputs.shape[1])
+        gate = []
+        if len(arrived) == 1:
+            gate = arrived[0]
+        elif arrived:
+            gate = parts[-2]
+        own, _ = lax.optimization_barrier((own, gate))
+        arrived.append(crossed(own, "col"))
+        parts.append(crossed(arrived[-1], "sub"))
     stages = bits_of(cycle)
-    held = [None] * PIECES
-    pending = [None] * PIECES
+    pieces = len(SHARES)
+    held = [None] * pieces
+    pending = [None] * pieces
     after = []
-    for turn in range(PIECES + len(stages)):
+    for turn in range(pieces + len(stages)):
         made = []
-        if turn < PIECES:
+        if turn < pieces:
             ready, _ = lax.optimization_barrier((parts[turn], after))
-            members = (order * local_rows + turn * height) // SEQ
+            span = slice(firsts[turn], firsts[turn] + SHARES[turn])
             product = piece_product(
-                jnp.concatenate(ready, axis=0), weight, factor_in, factor_out, members, height
+                jnp.concatenate(ready, axis=0), weight, projected[:, span], expanded[:, span]
             )
             pending[turn] = halves(product, stages[0], me, flip)
             made.append(pending[turn][0])
-        for j in range(min(turn, PIECES)):
+        for j in range(min(turn, pieces)):
             stage = turn - j - 1
             if stage >= len(stages):
                 continue

time: 249 us -> 215 us (0.86)
  local copies, waits for them, and re-layouts: 27.9 us -> 7.02 us
  waiting for transfers between devices: 105 us -> 89.1 us
  other arithmetic: 11.8 us -> 19.7 us
  matrix products: 81.4 us -> 73.9 us
  starting transfers between devices: 20.7 us -> 23.3 us
    unnamed x18 -> x8, local copies, waits for them, and re-layouts: 16.1 us -> 0.02 us
    ppermute x24 -> x27, waiting for transfers between devices: 105 us -> 89.1 us  [exchanged(): return lax.ppermute(block, axis, route)]
    dot_general x4 -> x1, matrix products: 10.3 us -> 3.09 us  [per_device(): jnp.einsum('buhf,buf->buh', inputs.reshape(per_shard, total_units, height...]
    reshape x0 -> x1, local copies, waits for them, and re-layouts: none -> 3.68 us  [per_device(): shaped[:, first * height:(first + share) * height]]
    gather x8 -> x2, local copies, waits for them, and re-layouts: 4.71 us -> 1.27 us  [the longest x1 0.65 us: per_device(): expanded = jnp.take(factor_out, members, axis=0).astype(jnp.float32)]
    another operation x1 -> x0, local copies, waits for them, and re-layouts: 3.2 us -> none  [per_device(): shaped[:, j].reshape(per_shard * height, inputs.shape[1])]
    concatenate x4 -> x0, local copies, waits for them, and re-layouts: 3.01 us -> none  [per_device(): jnp.concatenate(ready, axis=0)]
    div x8, other arithmetic: 0.8 us -> 3.75 us  [decode(): size = (jnp.log2(jnp.abs(code)) - FLOOR) * (scale / SPAN)]
  transfers between devices with their start and end apart: 24 -> 27, of which waited for: 9 -> 12; matrix products, arithmetic and copies ran while one was open for 41% -> 37% of each run, Pallas kernels for 0% -> 0%
where the time goes in v3:
time: 215 us
  waiting for transfers between devices  89.1 us (41%)
  matrix products  73.9 us (34%)
  starting transfers between devices  23.3 us (11%)
  other arithmetic  19.7 us (9%)
  local copies, waits for them, and re-layouts  7.02 us (3%)
    ppermute x27, waiting for transfers between devices, exchanged(): return lax.ppermute(block, axis, route)  89.1 us
    dot_general x4, matrix products, piece_product(): product = jnp.dot(rows, weight, preferred_element_type=jnp.float32)  56.2 us
    ppermute x27, starting transfers between devices, exchanged(): return lax.ppermute(block, axis, route)  23.3 us
    dot_general x1, matrix products, per_device(): lax.dot_general(left, right, (((0,), (0,)), ((), ())), preferred_element_...  14.6 us
  transfers between devices with their start and end apart: 27, of which 12 were waited for; matrix products, arithmetic and copies ran while one was open for 37% of the time, Pallas kernels for 0%

profile of v3, /device:TPU:0, one launch (start us, length us, event | category | flops | bytes accessed | tf_op | source)
XLA Modules:
  0.0 214.9 jit_solution(2536931892026603604)
XLA Ops:
  0.6 3.7 %slice_bitcast_fusion.1 = (bf16[64,7168]{1,0:T(8,128)(2,1)}, bf16[64,7168]{1,0:T(8,128)(2,1)}, bf16[64,7168]{1,0:T(8,128)(2,1)}, bf16[64,7168]{1,0:T(8,128)(2,1)S(1)}) fusion(bf16[1,256,7168]{2,1,0:T(8,128)(2,1)} %bitcast.112), kind=kLoop, calls=%fused_computation.108 | loop fusion | bytes 7340032 | tf_op jit(solution)/shard_map/reshape | solution.py:97
  4.3 2.9 %collective-permute-start.1 = (bf16[64,7168]{1,0:T(8,128)(2,1)S(1)}, bf16[64,7168]{1,0:T(8,128)(2,1)S(1)}, u32[]{:S(2)}, u32[]{:S(2)}) collective-permute-start(bf16[64,7168]{1,0:T(8,128)(2,1)S(1)} %get-tuple-element.21), channel_id=1, source_target_pairs={{0,2},{2,0},{1,3},{3,1},{4,6},{6,4},{5,7},{7,5},{8,10},{10,8},{9,1... | collective-permute-start | bytes 2752520 | tf_op jit(solution)/shard_map/ppermute | solution.py:38
  7.3 0.6 gather_fusion
  8.0 3.1 %fusion.103 = f32[8,1,32]{2,1,0:T(1,128)S(1)} fusion(bf16[8,32,7168]{2,1,0:T(8,128)(2,1)} %bitcast.113, bf16[8,7168,1]{1,0,2:T(8,128)(2,1)S(1)} %select_bitcast_fusion), kind=kOutput, calls=%fused_computation.172 | convolution fusion | flops 3670016 | bytes 3785728 | tf_op jit(solution)/shard_map/buhf,buf->buh/dot_general | solution.py:83
  11.2 0.5 collective-permute-start
  11.9 0.7 gather_fusion.1
  12.6 15.0 %collective-permute-done.1 = bf16[64,7168]{1,0:T(8,128)(2,1)S(1)} collective-permute-done((bf16[64,7168]{1,0:T(8,128)(2,1)S(1)}, bf16[64,7168]{1,0:T(8,128)(2,1)S(1)}, u32[]{:S(2)}, u32[]{:S(2)}) %collective-permute-start.1) | collective-permute-done | bytes 917536 | tf_op jit(solution)/shard_map/ppermute | solution.py:38
  27.9 0.6 collective-permute-start.5
  28.4 1.7 collective-permute-done.5
  30.2 1.7 collective-permute-start.9
  32.0 13.9 %fusion = f32[256,2048]{1,0:T(8,128)S(1)} fusion(bf16[7168,2048]{1,0:T(8,128)(2,1)} %param.7, bf16[64,7168]{1,0:T(8,128)(2,1)} %collective-permute-done.2, bf16[64,7168]{1,0:T(8,128)(2,1)S(1)} %collective-permute-done.1, bf16[64,7168]{1,0:T(8,128)(2,1)S(1)} %collective-permute-done, bf16[64,7168]{1,0:T(8,128)(2,1)S(1)} %get-tuple-element.21), kind=kOutput, calls=%fused_computation.3 | convolution fusion | flops 7530872832 | bytes 35127296 | tf_op jit(solution)/shard_map/dot_general | solution.py:54
  46.1 0.3 multiply_add_fusion
  46.5 0.4 fusion.49
  47.1 1.6 collective-permute-start.6
  48.8 0.6 collective-permute-start.14
  49.4 4.2 %collective-permute-done.9 = bf16[64,7168]{1,0:T(8,128)(2,1)} collective-permute-done((bf16[64,7168]{1,0:T(8,128)(2,1)}, bf16[64,7168]{1,0:T(8,128)(2,1)}, u32[]{:S(2)}, u32[]{:S(2)}) %collective-permute-start.9) | collective-permute-done | bytes 917536 | tf_op jit(solution)/shard_map/ppermute | solution.py:38
  53.6 8.1 %collective-permute-done.6 = bf16[2,64,2176]{2,1,0:T(8,128)(2,1)} collective-permute-done((bf16[2,64,2176]{2,1,0:T(8,128)(2,1)S(1)}, bf16[2,64,2176]{2,1,0:T(8,128)(2,1)}, u32[]{:S(2)}, u32[]{:S(2)}) %collective-permute-start.6) | collective-permute-done | bytes 557088 | tf_op jit(solution)/shard_map/ppermute | solution.py:38
  61.6 0.9 multiply_reduce_fusion.4
  62.5 1.5 fusion.50
  64.1 0.2 fusion.86
  64.4 13.9 %fusion.8 = f32[256,2048]{1,0:T(8,128)S(1)} fusion(bf16[7168,2048]{1,0:T(8,128)(2,1)} %param.7, bf16[64,7168]{1,0:T(8,128)(2,1)S(1)} %collective-permute-done.10, bf16[64,7168]{1,0:T(8,128)(2,1)} %collective-permute-done.9, bf16[64,7168]{1,0:T(8,128)(2,1)S(1)} %collective-permute-done.8, bf16[64,7168]{1,0:T(8,128)(2,1)} %get-tuple-element.26), kind=kOutput, calls=%fused_computation.11 | convolution fusion | flops 7530872832 | bytes 35127296 | tf_op jit(solution)/shard_map/dot_general | solution.py:54
  78.5 0.3 copy_add_fusion.2
  78.9 0.4 fusion.51
  79.4 0.9 pad_maximum_fusion.2
  80.3 1.6 collective-permute-start.11
  81.9 0.7 pad_maximum_fusion.5
  82.7 2.6 %collective-permute-start.7 = (bf16[1,64,2176]{2,1,0:T(8,128)(2,1)}, bf16[1,64,2176]{2,1,0:T(8,128)(2,1)}, u32[]{:S(2)}, u32[]{:S(2)}) collective-permute-start(bf16[1,64,2176]{2,1,0:T(8,128)(2,1)} %pad_maximum_fusion.5), channel_id=1, source_target_pairs={{0,8},{4,12},{8,0},{12,4},{1,9},{5,13},{9,1},{13,5},{2,10},{6,14},... | collective-permute-start | bytes 835592 | tf_op jit(solution)/shard_map/ppermute | solution.py:38
  85.4 13.7 %collective-permute-done.7 = bf16[1,64,2176]{2,1,0:T(8,128)(2,1)} collective-permute-done((bf16[1,64,2176]{2,1,0:T(8,128)(2,1)}, bf16[1,64,2176]{2,1,0:T(8,128)(2,1)}, u32[]{:S(2)}, u32[]{:S(2)}) %collective-permute-start.7) | collective-permute-done | bytes 278560 | tf_op jit(solution)/shard_map/ppermute | solution.py:38
  99.2 0.8 multiply_reduce_fusion.8
  100.0 0.6 collective-permute-start.19
  100.6 0.9 multiply_reduce_fusion.3
  101.5 1.5 fusion.52
  103.1 0.2 fusion.89
  103.5 3.4 %collective-permute-start.12 = (bf16[1,64,2176]{2,1,0:T(8,128)(2,1)S(1)}, bf16[1,64,2176]{2,1,0:T(8,128)(2,1)}, u32[]{:S(2)}, u32[]{:S(2)}) collective-permute-start(bf16[1,64,2176]{2,1,0:T(8,128)(2,1)S(1)} %pad_maximum_fusion.6), channel_id=1, source_target_pairs={{0,8},{4,12},{8,0},{12,4},{1,9},{5,13},{9,1},{13,5},{2,10},{6,14},... | collective-permute-start | bytes 835592 | tf_op jit(solution)/shard_map/ppermute | solution.py:38
  106.9 14.6 %fusion.16 = f32[256,2048]{1,0:T(8,128)S(1)} fusion(bf16[7168,2048]{1,0:T(8,128)(2,1)} %param.7, bf16[64,7168]{1,0:T(8,128)(2,1)} %collective-permute-done.15, bf16[64,7168]{1,0:T(8,128)(2,1)} %collective-permute-done.14, bf16[64,7168]{1,0:T(8,128)(2,1)} %collective-permute-done.13, bf16[64,7168]{1,0:T(8,128)(2,1)} %get-tuple-element.31), kind=kOutput, calls=%fused_computation.19 | convolution fusion | flops 7530872832 | bytes 35127296 | tf_op jit(solution)/shard_map/dot_general | solution.py:54
  121.7 0.3 copy_add_fusion.1
  122.2 0.4 fusion.53
  122.7 0.3 collective-permute-start.16
  123.1 1.2 fusion.88
  124.5 0.8 multiply_reduce_fusion.7
  125.3 0.4 collective-permute-start.20
  125.7 11.8 %collective-permute-done.16 = bf16[2,64,2176]{2,1,0:T(8,128)(2,1)S(1)} collective-permute-done((bf16[2,64,2176]{2,1,0:T(8,128)(2,1)S(1)}, bf16[2,64,2176]{2,1,0:T(8,128)(2,1)S(1)}, u32[]{:S(2)}, u32[]{:S(2)}) %collective-permute-start.16) | collective-permute-done | bytes 557088 | tf_op jit(solution)/shard_map/ppermute | solution.py:38
  137.7 0.4 fusion.54
  138.2 0.2 fusion.92
  138.6 1.4 collective-permute-start.17
  140.0 13.9 %fusion.24 = f32[256,2048]{1,0:T(8,128)S(1)} fusion(bf16[7168,2048]{1,0:T(8,128)(2,1)} %param.7, bf16[64,7168]{1,0:T(8,128)(2,1)} %collective-permute-done.20, bf16[64,7168]{1,0:T(8,128)(2,1)} %collective-permute-done.19, bf16[64,7168]{1,0:T(8,128)(2,1)S(1)} %collective-permute-done.18, bf16[64,7168]{1,0:T(8,128)(2,1)S(1)} %copy-done.3), kind=kOutput, calls=%fused_computation.27 | convolution fusion | flops 7530872832 | bytes 35127296 | tf_op jit(solution)/shard_map/dot_general | solution.py:54
  154.1 0.3 copy_add_fusion
  154.6 0.4 fusion.55
  155.1 1.8 collective-permute-start.21
  156.9 1.2 fusion.91
  158.2 10.9 %collective-permute-done.21 = bf16[2,64,2176]{2,1,0:T(8,128)(2,1)S(1)} collective-permute-done((bf16[2,64,2176]{2,1,0:T(8,128)(2,1)S(1)}, bf16[2,64,2176]{2,1,0:T(8,128)(2,1)S(1)}, u32[]{:S(2)}, u32[]{:S(2)}) %collective-permute-start.21) | collective-permute-done | bytes 557088 | tf_op jit(solution)/shard_map/ppermute | solution.py:38
  169.3 0.4 fusion.56
  169.9 0.2 fusion.95
  170.2 1.4 collective-permute-start.22
  171.8 12.4 %collective-permute-done.22 = bf16[1,64,2176]{2,1,0:T(8,128)(2,1)S(1)} collective-permute-done((bf16[1,64,2176]{2,1,0:T(8,128)(2,1)S(1)}, bf16[1,64,2176]{2,1,0:T(8,128)(2,1)S(1)}, u32[]{:S(2)}, u32[]{:S(2)}) %collective-permute-start.22) | collective-permute-done | bytes 278560 | tf_op jit(solution)/shard_map/ppermute | solution.py:38
  184.6 1.1 fusion.32
  185.7 0.4 multiply_reduce_fusion
  186.3 1.1 collective-permute-done.23
  187.4 1.5 collective-permute-start.24
  188.9 2.0 collective-permute-done.24
  190.9 3.5 %collective-permute-done.25 = f32[8]{0:T(128)S(1)} collective-permute-done((f32[8]{0:T(128)S(1)}, f32[8]{0:T(128)S(1)}, u32[]{:S(2)}, u32[]{:S(2)}) %collective-permute-start.25) | collective-permute-done | bytes 64 | tf_op jit(solution)/shard_map/ppermute | solution.py:38
  194.5 4.4 %collective-permute-done.26 = f32[8]{0:T(128)S(1)} collective-permute-done((f32[8]{0:T(128)S(1)}, f32[8]{0:T(128)S(1)}, u32[]{:S(2)}, u32[]{:S(2)}) %collective-permute-start.26) | collective-permute-done | bytes 64 | tf_op jit(solution)/shard_map/ppermute | solution.py:38
  198.9 0.6 fusion.132
  200.3 14.6 %convolution_convert_fusion = bf16[7168,2048]{1,0:T(8,128)(2,1)} fusion(bf16[8,7168]{1,0:T(8,128)(2,1)S(1)} %copy-done.1, bf16[8,2048]{1,0:T(8,128)(2,1)S(1)} %get-tuple-element.49, bf16[8,2048]{1,0:T(8,128)(2,1)S(1)} %get-tuple-element.50, bf16[8,2048]{1,0:T(8,128)(2,1)S(1)} %get-tuple-element.48), kind=kOutput, calls=%fused_computation.2 | convolution fusion | flops 720650240 | bytes 29573120 | tf_op jit(solution)/shard_map/dot_general | solution.py:155
  (102 shorter events, 5.4 us)
Async XLA Ops:
  0.6 6.7 %copy-start.1 = (bf16[8,7168]{1,0:T(8,128)(2,1)S(1)}, bf16[8,7168]{1,0:T(8,128)(2,1)}, u32[]{:S(2)}) copy-start(bf16[8,7168]{1,0:T(8,128)(2,1)} %param.8) | copy-start | bytes 344068
  4.3 23.3 %collective-permute-start.1 = (bf16[64,7168]{1,0:T(8,128)(2,1)S(1)}, bf16[64,7168]{1,0:T(8,128)(2,1)S(1)}, u32[]{:S(2)}, u32[]{:S(2)}) collective-permute-start(bf16[64,7168]{1,0:T(8,128)(2,1)S(1)} %get-tuple-element.21), channel_id=1, source_target_pairs={{0,2},{2,0},{1,3},{3,1},{4,6},{6,4},{5,7},{7,5},{8,10},{10,8},{9,1... | collective-permute-start | bytes 2752520 | tf_op jit(solution)/shard_map/ppermute | solution.py:38
  8.0 3.8 %copy-start = (bf16[8,2048]{1,0:T(8,128)(2,1)S(1)}, bf16[8,2048]{1,0:T(8,128)(2,1)}, u32[]{:S(2)}) copy-start(bf16[8,2048]{1,0:T(8,128)(2,1)} %param.9) | copy-start | bytes 98308
  11.1 16.7 %collective-permute-start.4 = (f32[1,8,32]{2,1,0:T(8,128)S(1)}, f32[1,8,32]{2,1,0:T(8,128)S(1)}, u32[]{:S(2)}, u32[]{:S(2)}) collective-permute-start(f32[1,8,32]{2,1,0:T(8,128)S(1)} %bitcast.118), channel_id=1, source_target_pairs={{0,2},{2,0},{1,3},{3,1},{4,6},{6,4},{5,7},{7,5},{8,10},{10,8},{9,1... | collective-permute-start | bytes 3080 | tf_op jit(solution)/shard_map/ppermute | solution.py:38
  11.1 17.3 %collective-permute-start.3 = (f32[1,8,32]{2,1,0:T(8,128)S(1)}, f32[1,8,32]{2,1,0:T(8,128)S(1)}, u32[]{:S(2)}, u32[]{:S(2)}) collective-permute-start(f32[1,8,32]{2,1,0:T(8,128)S(1)} %bitcast.119), channel_id=1, source_target_pairs={{0,1},{1,0},{2,3},{3,2},{4,5},{5,4},{6,7},{7,6},{8,9},{9,8},{10,11... | collective-permute-start | bytes 3080 | tf_op jit(solution)/shard_map/ppermute | solution.py:38
  11.2 20.8 %collective-permute-start = (bf16[64,7168]{1,0:T(8,128)(2,1)S(1)}, bf16[64,7168]{1,0:T(8,128)(2,1)S(1)}, u32[]{:S(2)}, u32[]{:S(2)}) collective-permute-start(bf16[64,7168]{1,0:T(8,128)(2,1)S(1)} %get-tuple-element.21), channel_id=1, source_target_pairs={{0,1},{1,0},{2,3},{3,2},{4,5},{5,4},{6,7},{7,6},{8,9},{9,8},{10,11... | collective-permute-start | bytes 2752520 | tf_op jit(solution)/shard_map/ppermute | solution.py:38
  27.6 4.3 %collective-permute-start.2 = (bf16[64,7168]{1,0:T(8,128)(2,1)S(1)}, bf16[64,7168]{1,0:T(8,128)(2,1)}, u32[]{:S(2)}, u32[]{:S(2)}) collective-permute-start(bf16[64,7168]{1,0:T(8,128)(2,1)S(1)} %collective-permute-done.1), channel_id=1, source_target_pairs={{0,1},{1,0},{2,3},{3,2},{4,5},{5,4},{6,7},{7,6},{8,9},{9,8},{10,11... | collective-permute-start | bytes 2752520 | tf_op jit(solution)/shard_map/ppermute | solution.py:38
  27.9 2.3 %collective-permute-start.5 = (f32[1,8,32]{2,1,0:T(8,128)S(1)}, f32[1,8,32]{2,1,0:T(8,128)S(1)}, u32[]{:S(2)}, u32[]{:S(2)}) collective-permute-start(f32[1,8,32]{2,1,0:T(8,128)S(1)} %collective-permute-done.4), channel_id=1, source_target_pairs={{0,1},{1,0},{2,3},{3,2},{4,5},{5,4},{6,7},{7,6},{8,9},{9,8},{10,11... | collective-permute-start | bytes 3080 | tf_op jit(solution)/shard_map/ppermute | solution.py:38
  30.2 23.4 %collective-permute-start.9 = (bf16[64,7168]{1,0:T(8,128)(2,1)}, bf16[64,7168]{1,0:T(8,128)(2,1)}, u32[]{:S(2)}, u32[]{:S(2)}) collective-permute-start(bf16[64,7168]{1,0:T(8,128)(2,1)} %get-tuple-element.26), channel_id=1, source_target_pairs={{0,2},{2,0},{1,3},{3,1},{4,6},{6,4},{5,7},{7,5},{8,10},{10,8},{9,1... | collective-permute-start | bytes 2752520 | tf_op jit(solution)/shard_map/ppermute | solution.py:38
  47.1 14.6 %collective-permute-start.6 = (bf16[2,64,2176]{2,1,0:T(8,128)(2,1)S(1)}, bf16[2,64,2176]{2,1,0:T(8,128)(2,1)}, u32[]{:S(2)}, u32[]{:S(2)}) collective-permute-start(bf16[2,64,2176]{2,1,0:T(8,128)(2,1)S(1)} %pad_maximum_fusion.1), channel_id=1, source_target_pairs={{0,4},{4,0},{8,12},{12,8},{1,5},{5,1},{9,13},{13,9},{2,6},{6,2},{1... | collective-permute-start | bytes 1671176 | tf_op jit(solution)/shard_map/ppermute | solution.py:38
  48.8 15.5 %collective-permute-start.8 = (bf16[64,7168]{1,0:T(8,128)(2,1)}, bf16[64,7168]{1,0:T(8,128)(2,1)S(1)}, u32[]{:S(2)}, u32[]{:S(2)}) collective-permute-start(bf16[64,7168]{1,0:T(8,128)(2,1)} %get-tuple-element.26), channel_id=1, source_target_pairs={{0,1},{1,0},{2,3},{3,2},{4,5},{5,4},{6,7},{7,6},{8,9},{9,8},{10,11... | collective-permute-start | bytes 2752520 | tf_op jit(solution)/shard_map/ppermute | solution.py:38
  48.8 51.8 %collective-permute-start.14 = (bf16[64,7168]{1,0:T(8,128)(2,1)}, bf16[64,7168]{1,0:T(8,128)(2,1)}, u32[]{:S(2)}, u32[]{:S(2)}) collective-permute-start(bf16[64,7168]{1,0:T(8,128)(2,1)} %get-tuple-element.31), channel_id=1, source_target_pairs={{0,2},{2,0},{1,3},{3,1},{4,6},{6,4},{5,7},{7,5},{8,10},{10,8},{9,1... | collective-permute-start | bytes 2752520 | tf_op jit(solution)/shard_map/ppermute | solution.py:38
  53.6 10.8 %collective-permute-start.10 = (bf16[64,7168]{1,0:T(8,128)(2,1)}, bf16[64,7168]{1,0:T(8,128)(2,1)S(1)}, u32[]{:S(2)}, u32[]{:S(2)}) collective-permute-start(bf16[64,7168]{1,0:T(8,128)(2,1)} %collective-permute-done.9), channel_id=1, source_target_pairs={{0,1},{1,0},{2,3},{3,2},{4,5},{5,4},{6,7},{7,6},{8,9},{9,8},{10,11... | collective-permute-start | bytes 2752520 | tf_op jit(solution)/shard_map/ppermute | solution.py:38
  80.3 20.3 %collective-permute-start.11 = (bf16[2,64,2176]{2,1,0:T(8,128)(2,1)}, bf16[2,64,2176]{2,1,0:T(8,128)(2,1)}, u32[]{:S(2)}, u32[]{:S(2)}) collective-permute-start(bf16[2,64,2176]{2,1,0:T(8,128)(2,1)} %pad_maximum_fusion.2), channel_id=1, source_target_pairs={{0,4},{4,0},{8,12},{12,8},{1,5},{5,1},{9,13},{13,9},{2,6},{6,2},{1... | collective-permute-start | bytes 1671176 | tf_op jit(solution)/shard_map/ppermute | solution.py:38
  82.7 16.5 %collective-permute-start.7 = (bf16[1,64,2176]{2,1,0:T(8,128)(2,1)}, bf16[1,64,2176]{2,1,0:T(8,128)(2,1)}, u32[]{:S(2)}, u32[]{:S(2)}) collective-permute-start(bf16[1,64,2176]{2,1,0:T(8,128)(2,1)} %pad_maximum_fusion.5), channel_id=1, source_target_pairs={{0,8},{4,12},{8,0},{12,4},{1,9},{5,13},{9,1},{13,5},{2,10},{6,14},... | collective-permute-start | bytes 835592 | tf_op jit(solution)/shard_map/ppermute | solution.py:38
  85.4 21.5 %collective-permute-start.13 = (bf16[64,7168]{1,0:T(8,128)(2,1)}, bf16[64,7168]{1,0:T(8,128)(2,1)}, u32[]{:S(2)}, u32[]{:S(2)}) collective-permute-start(bf16[64,7168]{1,0:T(8,128)(2,1)} %get-tuple-element.31), channel_id=1, source_target_pairs={{0,1},{1,0},{2,3},{3,2},{4,5},{5,4},{6,7},{7,6},{8,9},{9,8},{10,11... | collective-permute-start | bytes 2752520 | tf_op jit(solution)/shard_map/ppermute | solution.py:38
  100.0 25.3 %collective-permute-start.19 = (bf16[64,7168]{1,0:T(8,128)(2,1)}, bf16[64,7168]{1,0:T(8,128)(2,1)}, u32[]{:S(2)}, u32[]{:S(2)}) collective-permute-start(bf16[64,7168]{1,0:T(8,128)(2,1)} %get-tuple-element.36), channel_id=1, source_target_pairs={{0,2},{2,0},{1,3},{3,1},{4,6},{6,4},{5,7},{7,5},{8,10},{10,8},{9,1... | collective-permute-start | bytes 2752520 | tf_op jit(solution)/shard_map/ppermute | solution.py:38
  100.6 6.3 %collective-permute-start.15 = (bf16[64,7168]{1,0:T(8,128)(2,1)}, bf16[64,7168]{1,0:T(8,128)(2,1)}, u32[]{:S(2)}, u32[]{:S(2)}) collective-permute-start(bf16[64,7168]{1,0:T(8,128)(2,1)} %collective-permute-done.14), channel_id=1, source_target_pairs={{0,1},{1,0},{2,3},{3,2},{4,5},{5,4},{6,7},{7,6},{8,9},{9,8},{10,11... | collective-permute-start | bytes 2752520 | tf_op jit(solution)/shard_map/ppermute | solution.py:38
  103.5 21.0 %collective-permute-start.12 = (bf16[1,64,2176]{2,1,0:T(8,128)(2,1)S(1)}, bf16[1,64,2176]{2,1,0:T(8,128)(2,1)}, u32[]{:S(2)}, u32[]{:S(2)}) collective-permute-start(bf16[1,64,2176]{2,1,0:T(8,128)(2,1)S(1)} %pad_maximum_fusion.6), channel_id=1, source_target_pairs={{0,8},{4,12},{8,0},{12,4},{1,9},{5,13},{9,1},{13,5},{2,10},{6,14},... | collective-permute-start | bytes 835592 | tf_op jit(solution)/shard_map/ppermute | solution.py:38
  122.2 2.1 copy-start.3
  122.7 14.8 %collective-permute-start.16 = (bf16[2,64,2176]{2,1,0:T(8,128)(2,1)S(1)}, bf16[2,64,2176]{2,1,0:T(8,128)(2,1)S(1)}, u32[]{:S(2)}, u32[]{:S(2)}) collective-permute-start(bf16[2,64,2176]{2,1,0:T(8,128)(2,1)S(1)} %pad_maximum_fusion.3), channel_id=1, source_target_pairs={{0,4},{4,0},{8,12},{12,8},{1,5},{5,1},{9,13},{13,9},{2,6},{6,2},{1... | collective-permute-start | bytes 1671176 | tf_op jit(solution)/shard_map/ppermute | solution.py:38
  124.2 15.7 %collective-permute-start.18 = (bf16[64,7168]{1,0:T(8,128)(2,1)S(1)}, bf16[64,7168]{1,0:T(8,128)(2,1)S(1)}, u32[]{:S(2)}, u32[]{:S(2)}) collective-permute-start(bf16[64,7168]{1,0:T(8,128)(2,1)S(1)} %copy-done.3), channel_id=1, source_target_pairs={{0,1},{1,0},{2,3},{3,2},{4,5},{5,4},{6,7},{7,6},{8,9},{9,8},{10,11... | collective-permute-start | bytes 2752520 | tf_op jit(solution)/shard_map/ppermute | solution.py:38
  125.3 14.7 %collective-permute-start.20 = (bf16[64,7168]{1,0:T(8,128)(2,1)}, bf16[64,7168]{1,0:T(8,128)(2,1)}, u32[]{:S(2)}, u32[]{:S(2)}) collective-permute-start(bf16[64,7168]{1,0:T(8,128)(2,1)} %collective-permute-done.19), channel_id=1, source_target_pairs={{0,1},{1,0},{2,3},{3,2},{4,5},{5,4},{6,7},{7,6},{8,9},{9,8},{10,11... | collective-permute-start | bytes 2752520 | tf_op jit(solution)/shard_map/ppermute | solution.py:38
  138.6 19.5 %collective-permute-start.17 = (bf16[1,64,2176]{2,1,0:T(8,128)(2,1)S(1)}, bf16[1,64,2176]{2,1,0:T(8,128)(2,1)S(1)}, u32[]{:S(2)}, u32[]{:S(2)}) collective-permute-start(bf16[1,64,2176]{2,1,0:T(8,128)(2,1)S(1)} %pad_maximum_fusion.7), channel_id=1, source_target_pairs={{0,8},{4,12},{8,0},{12,4},{1,9},{5,13},{9,1},{13,5},{2,10},{6,14},... | collective-permute-start | bytes 835592 | tf_op jit(solution)/shard_map/ppermute | solution.py:38
  155.1 14.0 %collective-permute-start.21 = (bf16[2,64,2176]{2,1,0:T(8,128)(2,1)S(1)}, bf16[2,64,2176]{2,1,0:T(8,128)(2,1)S(1)}, u32[]{:S(2)}, u32[]{:S(2)}) collective-permute-start(bf16[2,64,2176]{2,1,0:T(8,128)(2,1)S(1)} %pad_maximum_fusion.4), channel_id=1, source_target_pairs={{0,4},{4,0},{8,12},{12,8},{1,5},{5,1},{9,13},{13,9},{2,6},{6,2},{1... | collective-permute-start | bytes 1671176 | tf_op jit(solution)/shard_map/ppermute | solution.py:38
  170.2 14.0 %collective-permute-start.22 = (bf16[1,64,2176]{2,1,0:T(8,128)(2,1)S(1)}, bf16[1,64,2176]{2,1,0:T(8,128)(2,1)S(1)}, u32[]{:S(2)}, u32[]{:S(2)}) collective-permute-start(bf16[1,64,2176]{2,1,0:T(8,128)(2,1)S(1)} %pad_maximum_fusion.8), channel_id=1, source_target_pairs={{0,8},{4,12},{8,0},{12,4},{1,9},{5,13},{9,1},{13,5},{2,10},{6,14},... | collective-permute-start | bytes 835592 | tf_op jit(solution)/shard_map/ppermute | solution.py:38
  184.3 1.4 copy-start.2
  186.2 1.2 collective-permute-start.23
  187.4 3.5 %collective-permute-start.24 = (f32[8]{0:T(128)S(1)}, f32[8]{0:T(128)S(1)}, u32[]{:S(2)}, u32[]{:S(2)}) collective-permute-start(f32[8]{0:T(128)S(1)} %add.335), channel_id=1, source_target_pairs={{0,2},{2,0},{1,3},{3,1},{4,6},{6,4},{5,7},{7,5},{8,10},{10,8},{9,1... | collective-permute-start | bytes 104 | tf_op jit(solution)/shard_map/ppermute | solution.py:38
  190.9 3.5 %collective-permute-start.25 = (f32[8]{0:T(128)S(1)}, f32[8]{0:T(128)S(1)}, u32[]{:S(2)}, u32[]{:S(2)}) collective-permute-start(f32[8]{0:T(128)S(1)} %add.336), channel_id=1, source_target_pairs={{0,4},{4,0},{8,12},{12,8},{1,5},{5,1},{9,13},{13,9},{2,6},{6,2},{1... | collective-permute-start | bytes 104 | tf_op jit(solution)/shard_map/ppermute | solution.py:38
  194.5 4.4 %collective-permute-start.26 = (f32[8]{0:T(128)S(1)}, f32[8]{0:T(128)S(1)}, u32[]{:S(2)}, u32[]{:S(2)}) collective-permute-start(f32[8]{0:T(128)S(1)} %add.337), channel_id=1, source_target_pairs={{0,8},{4,12},{8,0},{12,4},{1,9},{5,13},{9,1},{13,5},{2,10},{6,14},... | collective-permute-start | bytes 104 | tf_op jit(solution)/shard_map/ppermute | solution.py:38

commit v4 on v3

--- a/solution.py
+++ b/solution.py
@@ -9,7 +9,7 @@
 FF = 28672
 MEMBERS = 8
 SEQ = 128
-SHARES = (2, 2, 2, 2)
+SHARES = (2, 3, 2, 1)
 SPAN = 250.0
 FLOOR = -124.0
 
@@ -123,11 +123,14 @@
             if stage >= len(stages):
                 continue
             message, kept = pending[j]
-            held[j] = kept + decode(exchanged(message, "wide", stages[stage]))
+            received = exchanged(message, "wide", stages[stage])
+            if turn < pieces:
+                received, _ = lax.optimization_barrier((received, made[0]))
+            held[j] = kept + decode(received)
             if stage + 1 < len(stages):
                 pending[j] = halves(held[j], stages[stage + 1], me, flip)
                 made.append(pending[j][0])
-        after = made
+        after = made[:1]
     sums = [h[0] for h in held]
     perturbed = jnp.concatenate(sums, axis=0)
     outputs = perturbed.astype(jnp.bfloat16)

time: 215 us -> 222 us (1.033)
  local copies, waits for them, and re-layouts: 7.02 us -> 12.9 us
  waiting for transfers between devices: 89.1 us -> 93.1 us
  starting transfers between devices: 23.3 us -> 19.6 us
  matrix products: 73.9 us -> 77.5 us
  other arithmetic: 19.7 us -> 16.5 us
    ppermute x27, waiting for transfers between devices: 89.1 us -> 93.1 us  [exchanged(): return lax.ppermute(block, axis, route)]
    ppermute x27, starting transfers between devices: 23.3 us -> 19.6 us  [exchanged(): return lax.ppermute(block, axis, route)]
    dot_general x4, matrix products: 56.2 us -> 59.7 us  [piece_product(): product = jnp.dot(rows, weight, preferred_element_type=jnp.float32)]
where the time goes in v4:
time: 222 us
  waiting for transfers between devices  93.1 us (42%)
  matrix products  77.5 us (35%)
  starting transfers between devices  19.6 us (9%)
  other arithmetic  16.5 us (7%)
  local copies, waits for them, and re-layouts  12.9 us (6%)
    ppermute x27, waiting for transfers between devices, exchanged(): return lax.ppermute(block, axis, route)  93.1 us
    dot_general x4, matrix products, piece_product(): product = jnp.dot(rows, weight, preferred_element_type=jnp.float32)  59.7 us
    ppermute x27, starting transfers between devices, exchanged(): return lax.ppermute(block, axis, route)  19.6 us
    dot_general x1, matrix products, per_device(): lax.dot_general(left, right, (((0,), (0,)), ((), ())), preferred_element_...  14.6 us
  transfers between devices with their start and end apart: 27, of which 12 were waited for; matrix products, arithmetic and copies ran while one was open for 37% of the time, Pallas kernels for 0%

profile of v4, /device:TPU:0, one launch (start us, length us, event | category | flops | bytes accessed | tf_op | source)
XLA Modules:
  0.0 221.6 jit_solution(16539906087150493311)
XLA Ops:
  0.7 1.6 gather_fusion
  2.4 3.2 %convolution_bitcast_fusion = f32[1,8,32]{2,0,1:T(1,128)S(1)} fusion(bf16[8,32,7168]{2,1,0:T(8,128)(2,1)} %bitcast.120, bf16[8,7168,1]{1,0,2:T(8,128)(2,1)S(1)} %select_bitcast_fusion), kind=kOutput, calls=%fused_computation.70 | convolution fusion | flops 3670016 | bytes 3785728 | tf_op jit(solution)/shard_map/buhf,buf->buh/dot_general | solution.py:83
  5.7 3.0 %collective-permute-start.4 = (f32[1,8,32]{2,0,1:T(1,128)S(1)}, f32[1,8,32]{2,0,1:T(1,128)S(1)}, u32[]{:S(2)}, u32[]{:S(2)}) collective-permute-start(f32[1,8,32]{2,0,1:T(1,128)S(1)} %convolution_bitcast_fusion), channel_id=1, source_target_pairs={{0,2},{2,0},{1,3},{3,1},{4,6},{6,4},{5,7},{7,5},{8,10},{10,8},{9,1... | collective-permute-start | bytes 3080 | tf_op jit(solution)/shard_map/ppermute | solution.py:38
  8.6 1.0 slice_bitcast_fusion.1
  9.7 0.5 collective-permute-start
  10.4 1.9 slice_bitcast_fusion.3
  12.2 1.4 slice_bitcast_fusion
  13.8 0.7 gather_fusion.1
  14.5 0.7 fusion.133
  15.2 17.4 %collective-permute-done.1 = bf16[64,7168]{1,0:T(8,128)(2,1)} collective-permute-done((bf16[64,7168]{1,0:T(8,128)(2,1)S(1)}, bf16[64,7168]{1,0:T(8,128)(2,1)}, u32[]{:S(2)}, u32[]{:S(2)}) %collective-permute-start.1) | collective-permute-done | bytes 917536 | tf_op jit(solution)/shard_map/ppermute | solution.py:38
  32.6 0.6 and_select_fusion
  33.3 0.6 collective-permute-start.5
  33.9 0.7 slice.121
  34.7 0.4 collective-permute-done.5
  35.4 0.3 collective-permute-start.8
  35.7 1.8 collective-permute-start.12
  37.7 14.1 %fusion.8 = f32[256,2048]{1,0:T(8,128)S(1)} fusion(bf16[7168,2048]{1,0:T(8,128)(2,1)} %param.7, bf16[64,7168]{1,0:T(8,128)(2,1)} %collective-permute-done.2, bf16[64,7168]{1,0:T(8,128)(2,1)} %collective-permute-done.1, bf16[64,7168]{1,0:T(8,128)(2,1)} %collective-permute-done, bf16[64,7168]{1,0:T(8,128)(2,1)S(1)} %get-tuple-element.26), kind=kOutput, calls=%fused_computation.11 | convolution fusion | flops 7530872832 | bytes 35127296 | tf_op jit(solution)/shard_map/dot_general | solution.py:54
  51.8 16.7 %collective-permute-done.8 = bf16[96,7168]{1,0:T(8,128)(2,1)S(1)} collective-permute-done((bf16[96,7168]{1,0:T(8,128)(2,1)S(1)}, bf16[96,7168]{1,0:T(8,128)(2,1)S(1)}, u32[]{:S(2)}, u32[]{:S(2)}) %collective-permute-start.8) | collective-permute-done | bytes 1376288 | tf_op jit(solution)/shard_map/ppermute | solution.py:38
  68.7 0.3 multiply_add_fusion.1
  69.2 0.4 fusion.51
  69.7 0.9 pad_maximum_fusion.2
  70.5 1.6 collective-permute-start.6
  72.1 15.3 %collective-permute-done.12 = bf16[64,7168]{1,0:T(8,128)(2,1)} collective-permute-done((bf16[64,7168]{1,0:T(8,128)(2,1)}, bf16[64,7168]{1,0:T(8,128)(2,1)}, u32[]{:S(2)}, u32[]{:S(2)}) %collective-permute-start.12) | collective-permute-done | bytes 917536 | tf_op jit(solution)/shard_map/ppermute | solution.py:38
  87.4 1.1 copy-done.8
  88.5 0.3 collective-permute-start.17
  89.0 19.1 %fusion = f32[384,2048]{1,0:T(8,128)} fusion(bf16[7168,2048]{1,0:T(8,128)(2,1)} %param.7, bf16[96,7168]{1,0:T(8,128)(2,1)} %copy-done.8, bf16[96,7168]{1,0:T(8,128)(2,1)} %copy-done.7, bf16[96,7168]{1,0:T(8,128)(2,1)} %collective-permute-done.7, bf16[96,7168]{1,0:T(8,128)(2,1)S(1)} %slice_bitcast_fusion), kind=kOutput, calls=%fused_computation.3 | convolution fusion | flops 11296309248 | bytes 38010880 | tf_op jit(solution)/shard_map/dot_general | solution.py:54
  108.1 1.4 mul.437
  109.5 0.5 copy-done.3
  110.1 0.4 multiply_add_fusion
  110.7 0.6 fusion.36
  111.4 1.9 collective-permute-start.14
  113.3 0.9 multiply_reduce_fusion.3
  114.2 1.4 fusion.52
  115.8 14.6 %fusion.16 = f32[256,2048]{1,0:T(8,128)S(1)} fusion(bf16[7168,2048]{1,0:T(8,128)(2,1)} %param.7, bf16[64,7168]{1,0:T(8,128)(2,1)} %collective-permute-done.13, bf16[64,7168]{1,0:T(8,128)(2,1)} %collective-permute-done.12, bf16[64,7168]{1,0:T(8,128)(2,1)} %collective-permute-done.11, bf16[64,7168]{1,0:T(8,128)(2,1)} %get-tuple-element.37), kind=kOutput, calls=%fused_computation.19 | convolution fusion | flops 7530872832 | bytes 35127296 | tf_op jit(solution)/shard_map/dot_general | solution.py:54
  130.6 0.3 copy_add_fusion
  131.1 0.2 fusion.81
  131.4 2.7 %collective-permute-start.10 = (bf16[1,64,2176]{2,1,0:T(8,128)(2,1)S(1)}, bf16[1,64,2176]{2,1,0:T(8,128)(2,1)S(1)}, u32[]{:S(2)}, u32[]{:S(2)}) collective-permute-start(bf16[1,64,2176]{2,1,0:T(8,128)(2,1)S(1)} %pad_maximum_fusion.5), channel_id=1, source_target_pairs={{0,8},{4,12},{8,0},{12,4},{1,9},{5,13},{9,1},{13,5},{2,10},{6,14},... | collective-permute-start | bytes 835592 | tf_op jit(solution)/shard_map/ppermute | solution.py:38
  134.1 0.4 fusion.53
  134.6 0.5 collective-permute-start.19
  135.1 11.7 %collective-permute-done.10 = bf16[1,64,2176]{2,1,0:T(8,128)(2,1)S(1)} collective-permute-done((bf16[1,64,2176]{2,1,0:T(8,128)(2,1)S(1)}, bf16[1,64,2176]{2,1,0:T(8,128)(2,1)S(1)}, u32[]{:S(2)}, u32[]{:S(2)}) %collective-permute-start.10) | collective-permute-done | bytes 278560 | tf_op jit(solution)/shard_map/ppermute | solution.py:38
  147.0 0.2 fusion.83
  147.3 0.9 multiply_reduce_fusion.1
  148.2 1.7 fusion.37
  150.2 0.3 fusion.66
  150.7 11.8 %fusion.24 = f32[128,2048]{1,0:T(8,128)S(1)} fusion(bf16[7168,2048]{1,0:T(8,128)(2,1)} %param.7, bf16[32,7168]{1,0:T(8,128)(2,1)S(1)} %collective-permute-done.18, bf16[32,7168]{1,0:T(8,128)(2,1)} %collective-permute-done.17, bf16[32,7168]{1,0:T(8,128)(2,1)} %collective-permute-done.16, bf16[32,7168]{1,0:T(8,128)(2,1)} %slice_bitcast_fusion.3), kind=kOutput, calls=%fused_computation.37 | convolution fusion | flops 3765436416 | bytes 32243712 | tf_op jit(solution)/shard_map/dot_general | solution.py:54
  162.9 0.2 fusion.84
  163.2 3.3 %collective-permute-start.21 = (bf16[2,32,2176]{2,1,0:T(8,128)(2,1)S(1)}, bf16[2,32,2176]{2,1,0:T(8,128)(2,1)S(1)}, u32[]{:S(2)}, u32[]{:S(2)}) collective-permute-start(bf16[2,32,2176]{2,1,0:T(8,128)(2,1)S(1)} %pad_maximum_fusion.6), channel_id=1, source_target_pairs={{0,4},{4,0},{8,12},{12,8},{1,5},{5,1},{9,13},{13,9},{2,6},{6,2},{1... | collective-permute-start | bytes 835592 | tf_op jit(solution)/shard_map/ppermute | solution.py:38
  166.6 0.4 fusion.54
  167.2 0.2 fusion.85
  167.6 12.8 %collective-permute-done.21 = bf16[2,32,2176]{2,1,0:T(8,128)(2,1)S(1)} collective-permute-done((bf16[2,32,2176]{2,1,0:T(8,128)(2,1)S(1)}, bf16[2,32,2176]{2,1,0:T(8,128)(2,1)S(1)}, u32[]{:S(2)}, u32[]{:S(2)}) %collective-permute-start.21) | collective-permute-done | bytes 278560 | tf_op jit(solution)/shard_map/ppermute | solution.py:38
  181.1 0.9 collective-permute-start.22
  182.0 2.6 %collective-permute-done.20 = bf16[1,64,2176]{2,1,0:T(8,128)(2,1)S(1)} collective-permute-done((bf16[1,64,2176]{2,1,0:T(8,128)(2,1)S(1)}, bf16[1,64,2176]{2,1,0:T(8,128)(2,1)S(1)}, u32[]{:S(2)}, u32[]{:S(2)}) %collective-permute-start.20) | collective-permute-done | bytes 278560 | tf_op jit(solution)/shard_map/ppermute | solution.py:38
  185.0 0.3 fusion.68
  185.3 5.4 %collective-permute-done.22 = bf16[1,32,2176]{2,1,0:T(8,128)(2,1)S(1)} collective-permute-done((bf16[1,32,2176]{2,1,0:T(8,128)(2,1)S(1)}, bf16[1,32,2176]{2,1,0:T(8,128)(2,1)S(1)}, u32[]{:S(2)}, u32[]{:S(2)}) %collective-permute-start.22) | collective-permute-done | bytes 139296 | tf_op jit(solution)/shard_map/ppermute | solution.py:38
  191.0 1.1 fusion.42
  192.1 0.4 multiply_reduce_fusion
  192.4 0.3 copy-done.6
  192.9 1.1 collective-permute-done.23
  194.1 1.5 collective-permute-start.24
  195.6 2.0 collective-permute-done.24
  197.6 3.5 %collective-permute-done.25 = f32[8]{0:T(128)S(1)} collective-permute-done((f32[8]{0:T(128)S(1)}, f32[8]{0:T(128)S(1)}, u32[]{:S(2)}, u32[]{:S(2)}) %collective-permute-start.25) | collective-permute-done | bytes 64 | tf_op jit(solution)/shard_map/ppermute | solution.py:38
  201.4 4.2 %collective-permute-done.26 = f32[8]{0:T(128)S(1)} collective-permute-done((f32[8]{0:T(128)S(1)}, f32[8]{0:T(128)S(1)}, u32[]{:S(2)}, u32[]{:S(2)}) %collective-permute-start.26) | collective-permute-done | bytes 64 | tf_op jit(solution)/shard_map/ppermute | solution.py:38
  205.6 0.6 fusion.132
  207.0 14.6 %convolution_convert_fusion = bf16[7168,2048]{1,0:T(8,128)(2,1)} fusion(bf16[8,7168]{1,0:T(8,128)(2,1)S(1)} %copy-done.1, bf16[8,2048]{1,0:T(8,128)(2,1)S(1)} %get-tuple-element.55, bf16[8,2048]{1,0:T(8,128)(2,1)S(1)} %get-tuple-element.56, bf16[8,2048]{1,0:T(8,128)(2,1)S(1)} %get-tuple-element.54), kind=kOutput, calls=%fused_computation.2 | convolution fusion | flops 720650240 | bytes 29573120 | tf_op jit(solution)/shard_map/dot_general | solution.py:158
  (120 shorter events, 6.2 us)
Async XLA Ops:
  2.4 6.2 %copy-start.2 = (bf16[256,7168]{1,0:T(8,128)(2,1)S(1)}, bf16[256,7168]{1,0:T(8,128)(2,1)}, u32[]{:S(2)}) copy-start(bf16[256,7168]{1,0:T(8,128)(2,1)} %param.5) | copy-start | bytes 11010052
  5.7 27.6 %collective-permute-start.4 = (f32[1,8,32]{2,0,1:T(1,128)S(1)}, f32[1,8,32]{2,0,1:T(1,128)S(1)}, u32[]{:S(2)}, u32[]{:S(2)}) collective-permute-start(f32[1,8,32]{2,0,1:T(1,128)S(1)} %convolution_bitcast_fusion), channel_id=1, source_target_pairs={{0,2},{2,0},{1,3},{3,1},{4,6},{6,4},{5,7},{7,5},{8,10},{10,8},{9,1... | collective-permute-start | bytes 3080 | tf_op jit(solution)/shard_map/ppermute | solution.py:38
  8.6 26.0 %collective-permute-start.3 = (f32[1,8,32]{2,0,1:T(1,128)S(1)}, f32[1,8,32]{2,0,1:T(1,128)S(1)}, u32[]{:S(2)}, u32[]{:S(2)}) collective-permute-start(f32[1,8,32]{2,0,1:T(1,128)S(1)} %convolution_bitcast_fusion), channel_id=1, source_target_pairs={{0,1},{1,0},{2,3},{3,2},{4,5},{5,4},{6,7},{7,6},{8,9},{9,8},{10,11... | collective-permute-start | bytes 3080 | tf_op jit(solution)/shard_map/ppermute | solution.py:38
  9.7 4.1 %copy-start = (bf16[8,2048]{1,0:T(8,128)(2,1)S(1)}, bf16[8,2048]{1,0:T(8,128)(2,1)}, u32[]{:S(2)}) copy-start(bf16[8,2048]{1,0:T(8,128)(2,1)} %param.9) | copy-start | bytes 98308
  9.7 22.9 %collective-permute-start.1 = (bf16[64,7168]{1,0:T(8,128)(2,1)S(1)}, bf16[64,7168]{1,0:T(8,128)(2,1)}, u32[]{:S(2)}, u32[]{:S(2)}) collective-permute-start(bf16[64,7168]{1,0:T(8,128)(2,1)S(1)} %get-tuple-element.26), channel_id=1, source_target_pairs={{0,2},{2,0},{1,3},{3,1},{4,6},{6,4},{5,7},{7,5},{8,10},{10,8},{9,1... | collective-permute-start | bytes 2752520 | tf_op jit(solution)/shard_map/ppermute | solution.py:38
  9.7 25.9 %collective-permute-start = (bf16[64,7168]{1,0:T(8,128)(2,1)S(1)}, bf16[64,7168]{1,0:T(8,128)(2,1)}, u32[]{:S(2)}, u32[]{:S(2)}) collective-permute-start(bf16[64,7168]{1,0:T(8,128)(2,1)S(1)} %get-tuple-element.26), channel_id=1, source_target_pairs={{0,1},{1,0},{2,3},{3,2},{4,5},{5,4},{6,7},{7,6},{8,9},{9,8},{10,11... | collective-permute-start | bytes 2752520 | tf_op jit(solution)/shard_map/ppermute | solution.py:38
  32.6 3.1 %collective-permute-start.2 = (bf16[64,7168]{1,0:T(8,128)(2,1)}, bf16[64,7168]{1,0:T(8,128)(2,1)}, u32[]{:S(2)}, u32[]{:S(2)}) collective-permute-start(bf16[64,7168]{1,0:T(8,128)(2,1)} %collective-permute-done.1), channel_id=1, source_target_pairs={{0,1},{1,0},{2,3},{3,2},{4,5},{5,4},{6,7},{7,6},{8,9},{9,8},{10,11... | collective-permute-start | bytes 2752520 | tf_op jit(solution)/shard_map/ppermute | solution.py:38
  33.3 1.7 collective-permute-start.5
  35.4 33.0 %collective-permute-start.8 = (bf16[96,7168]{1,0:T(8,128)(2,1)S(1)}, bf16[96,7168]{1,0:T(8,128)(2,1)S(1)}, u32[]{:S(2)}, u32[]{:S(2)}) collective-permute-start(bf16[96,7168]{1,0:T(8,128)(2,1)S(1)} %slice_bitcast_fusion), channel_id=1, source_target_pairs={{0,2},{2,0},{1,3},{3,1},{4,6},{6,4},{5,7},{7,5},{8,10},{10,8},{9,1... | collective-permute-start | bytes 4128776 | tf_op jit(solution)/shard_map/ppermute | solution.py:38
  35.7 51.7 %collective-permute-start.7 = (bf16[96,7168]{1,0:T(8,128)(2,1)S(1)}, bf16[96,7168]{1,0:T(8,128)(2,1)}, u32[]{:S(2)}, u32[]{:S(2)}) collective-permute-start(bf16[96,7168]{1,0:T(8,128)(2,1)S(1)} %slice_bitcast_fusion), channel_id=1, source_target_pairs={{0,1},{1,0},{2,3},{3,2},{4,5},{5,4},{6,7},{7,6},{8,9},{9,8},{10,11... | collective-permute-start | bytes 4128776 | tf_op jit(solution)/shard_map/ppermute | solution.py:38
  35.7 51.7 %collective-permute-start.12 = (bf16[64,7168]{1,0:T(8,128)(2,1)}, bf16[64,7168]{1,0:T(8,128)(2,1)}, u32[]{:S(2)}, u32[]{:S(2)}) collective-permute-start(bf16[64,7168]{1,0:T(8,128)(2,1)} %get-tuple-element.37), channel_id=1, source_target_pairs={{0,2},{2,0},{1,3},{3,1},{4,6},{6,4},{5,7},{7,5},{8,10},{10,8},{9,1... | collective-permute-start | bytes 2752520 | tf_op jit(solution)/shard_map/ppermute | solution.py:38
  37.5 73.9 %collective-permute-start.11 = (bf16[64,7168]{1,0:T(8,128)(2,1)}, bf16[64,7168]{1,0:T(8,128)(2,1)}, u32[]{:S(2)}, u32[]{:S(2)}) collective-permute-start(bf16[64,7168]{1,0:T(8,128)(2,1)} %get-tuple-element.37), channel_id=1, source_target_pairs={{0,1},{1,0},{2,3},{3,2},{4,5},{5,4},{6,7},{7,6},{8,9},{9,8},{10,11... | collective-permute-start | bytes 2752520 | tf_op jit(solution)/shard_map/ppermute | solution.py:38
  68.4 19.0 %copy-start.7 = (bf16[96,7168]{1,0:T(8,128)(2,1)}, bf16[96,7168]{1,0:T(8,128)(2,1)S(1)}, u32[]{:S(2)}) copy-start(bf16[96,7168]{1,0:T(8,128)(2,1)S(1)} %collective-permute-done.8) | copy-start | bytes 4128772
  68.4 19.0 %collective-permute-start.9 = (bf16[96,7168]{1,0:T(8,128)(2,1)S(1)}, bf16[96,7168]{1,0:T(8,128)(2,1)S(1)}, u32[]{:S(2)}, u32[]{:S(2)}) collective-permute-start(bf16[96,7168]{1,0:T(8,128)(2,1)S(1)} %collective-permute-done.8), channel_id=1, source_target_pairs={{0,1},{1,0},{2,3},{3,2},{4,5},{5,4},{6,7},{7,6},{8,9},{9,8},{10,11... | collective-permute-start | bytes 4128776 | tf_op jit(solution)/shard_map/ppermute | solution.py:38
  70.5 42.8 %collective-permute-start.6 = (bf16[2,64,2176]{2,1,0:T(8,128)(2,1)}, bf16[2,64,2176]{2,1,0:T(8,128)(2,1)}, u32[]{:S(2)}, u32[]{:S(2)}) collective-permute-start(bf16[2,64,2176]{2,1,0:T(8,128)(2,1)} %pad_maximum_fusion.2), channel_id=1, source_target_pairs={{0,4},{4,0},{8,12},{12,8},{1,5},{5,1},{9,13},{13,9},{2,6},{6,2},{1... | collective-permute-start | bytes 1671176 | tf_op jit(solution)/shard_map/ppermute | solution.py:38
  87.4 25.9 %collective-permute-start.13 = (bf16[64,7168]{1,0:T(8,128)(2,1)}, bf16[64,7168]{1,0:T(8,128)(2,1)}, u32[]{:S(2)}, u32[]{:S(2)}) collective-permute-start(bf16[64,7168]{1,0:T(8,128)(2,1)} %collective-permute-done.12), channel_id=1, source_target_pairs={{0,1},{1,0},{2,3},{3,2},{4,5},{5,4},{6,7},{7,6},{8,9},{9,8},{10,11... | collective-permute-start | bytes 2752520 | tf_op jit(solution)/shard_map/ppermute | solution.py:38
  87.4 1.1 copy-start.8
  88.5 58.8 %collective-permute-start.17 = (bf16[32,7168]{1,0:T(8,128)(2,1)}, bf16[32,7168]{1,0:T(8,128)(2,1)}, u32[]{:S(2)}, u32[]{:S(2)}) collective-permute-start(bf16[32,7168]{1,0:T(8,128)(2,1)} %slice_bitcast_fusion.3), channel_id=1, source_target_pairs={{0,2},{2,0},{1,3},{3,1},{4,6},{6,4},{5,7},{7,5},{8,10},{10,8},{9,1... | collective-permute-start | bytes 1376264 | tf_op jit(solution)/shard_map/ppermute | solution.py:38
  88.8 61.9 %collective-permute-start.16 = (bf16[32,7168]{1,0:T(8,128)(2,1)}, bf16[32,7168]{1,0:T(8,128)(2,1)}, u32[]{:S(2)}, u32[]{:S(2)}) collective-permute-start(bf16[32,7168]{1,0:T(8,128)(2,1)} %slice_bitcast_fusion.3), channel_id=1, source_target_pairs={{0,1},{1,0},{2,3},{3,2},{4,5},{5,4},{6,7},{7,6},{8,9},{9,8},{10,11... | collective-permute-start | bytes 1376264 | tf_op jit(solution)/shard_map/ppermute | solution.py:38
  108.1 2.0 copy-start.3
  111.4 35.9 %collective-permute-start.14 = (bf16[2,96,2176]{2,1,0:T(8,128)(2,1)S(1)}, bf16[2,96,2176]{2,1,0:T(8,128)(2,1)}, u32[]{:S(2)}, u32[]{:S(2)}) collective-permute-start(bf16[2,96,2176]{2,1,0:T(8,128)(2,1)S(1)} %pad_maximum_fusion.1), channel_id=1, source_target_pairs={{0,4},{4,0},{8,12},{12,8},{1,5},{5,1},{9,13},{13,9},{2,6},{6,2},{1... | collective-permute-start | bytes 2506760 | tf_op jit(solution)/shard_map/ppermute | solution.py:38
  115.8 14.6 %copy-start.5 = (f32[4,2,2048]{2,1,0:T(2,128)S(1)}, f32[4,2,2048]{2,1,0:T(2,128)}, u32[]{:S(2)}) copy-start(f32[4,2,2048]{2,1,0:T(2,128)} %get-tuple-element.52) | copy-start | bytes 196612
  131.4 15.5 %collective-permute-start.10 = (bf16[1,64,2176]{2,1,0:T(8,128)(2,1)S(1)}, bf16[1,64,2176]{2,1,0:T(8,128)(2,1)S(1)}, u32[]{:S(2)}, u32[]{:S(2)}) collective-permute-start(bf16[1,64,2176]{2,1,0:T(8,128)(2,1)S(1)} %pad_maximum_fusion.5), channel_id=1, source_target_pairs={{0,8},{4,12},{8,0},{12,4},{1,9},{5,13},{9,1},{13,5},{2,10},{6,14},... | collective-permute-start | bytes 835592 | tf_op jit(solution)/shard_map/ppermute | solution.py:38
  134.6 31.9 %collective-permute-start.19 = (bf16[2,64,2176]{2,1,0:T(8,128)(2,1)S(1)}, bf16[2,64,2176]{2,1,0:T(8,128)(2,1)S(1)}, u32[]{:S(2)}, u32[]{:S(2)}) collective-permute-start(bf16[2,64,2176]{2,1,0:T(8,128)(2,1)S(1)} %pad_maximum_fusion.3), channel_id=1, source_target_pairs={{0,4},{4,0},{8,12},{12,8},{1,5},{5,1},{9,13},{13,9},{2,6},{6,2},{1... | collective-permute-start | bytes 1671176 | tf_op jit(solution)/shard_map/ppermute | solution.py:38
  147.2 3.4 %collective-permute-start.18 = (bf16[32,7168]{1,0:T(8,128)(2,1)}, bf16[32,7168]{1,0:T(8,128)(2,1)S(1)}, u32[]{:S(2)}, u32[]{:S(2)}) collective-permute-start(bf16[32,7168]{1,0:T(8,128)(2,1)} %collective-permute-done.17), channel_id=1, source_target_pairs={{0,1},{1,0},{2,3},{3,2},{4,5},{5,4},{6,7},{7,6},{8,9},{9,8},{10,11... | collective-permute-start | bytes 1376264 | tf_op jit(solution)/shard_map/ppermute | solution.py:38
  150.6 34.3 %collective-permute-start.15 = (bf16[1,96,2176]{2,1,0:T(8,128)(2,1)S(1)}, bf16[1,96,2176]{2,1,0:T(8,128)(2,1)S(1)}, u32[]{:S(2)}, u32[]{:S(2)}) collective-permute-start(bf16[1,96,2176]{2,1,0:T(8,128)(2,1)S(1)} %pad_maximum_fusion.4), channel_id=1, source_target_pairs={{0,8},{4,12},{8,0},{12,4},{1,9},{5,13},{9,1},{13,5},{2,10},{6,14},... | collective-permute-start | bytes 1253384 | tf_op jit(solution)/shard_map/ppermute | solution.py:38
  163.2 17.2 %collective-permute-start.21 = (bf16[2,32,2176]{2,1,0:T(8,128)(2,1)S(1)}, bf16[2,32,2176]{2,1,0:T(8,128)(2,1)S(1)}, u32[]{:S(2)}, u32[]{:S(2)}) collective-permute-start(bf16[2,32,2176]{2,1,0:T(8,128)(2,1)S(1)} %pad_maximum_fusion.6), channel_id=1, source_target_pairs={{0,4},{4,0},{8,12},{12,8},{1,5},{5,1},{9,13},{13,9},{2,6},{6,2},{1... | collective-permute-start | bytes 835592 | tf_op jit(solution)/shard_map/ppermute | solution.py:38
  167.5 17.0 %collective-permute-start.20 = (bf16[1,64,2176]{2,1,0:T(8,128)(2,1)S(1)}, bf16[1,64,2176]{2,1,0:T(8,128)(2,1)S(1)}, u32[]{:S(2)}, u32[]{:S(2)}) collective-permute-start(bf16[1,64,2176]{2,1,0:T(8,128)(2,1)S(1)} %pad_maximum_fusion.7), channel_id=1, source_target_pairs={{0,8},{4,12},{8,0},{12,4},{1,9},{5,13},{9,1},{13,5},{2,10},{6,14},... | collective-permute-start | bytes 835592 | tf_op jit(solution)/shard_map/ppermute | solution.py:38
  181.1 9.6 %collective-permute-start.22 = (bf16[1,32,2176]{2,1,0:T(8,128)(2,1)S(1)}, bf16[1,32,2176]{2,1,0:T(8,128)(2,1)S(1)}, u32[]{:S(2)}, u32[]{:S(2)}) collective-permute-start(bf16[1,32,2176]{2,1,0:T(8,128)(2,1)S(1)} %pad_maximum_fusion.8), channel_id=1, source_target_pairs={{0,8},{4,12},{8,0},{12,4},{1,9},{5,13},{9,1},{13,5},{2,10},{6,14},... | collective-permute-start | bytes 417800 | tf_op jit(solution)/shard_map/ppermute | solution.py:38
  185.3 6.8 %copy-start.4 = (bf16[256,2048]{1,0:T(8,128)(2,1)S(1)}, bf16[256,2048]{1,0:T(8,128)(2,1)}, u32[]{:S(2)}) copy-start(bf16[256,2048]{1,0:T(8,128)(2,1)} %param.6) | copy-start | bytes 3145732
  192.1 0.7 copy-start.6
  192.1 14.9 %copy-start.1 = (bf16[8,7168]{1,0:T(8,128)(2,1)S(1)}, bf16[8,7168]{1,0:T(8,128)(2,1)}, u32[]{:S(2)}) copy-start(bf16[8,7168]{1,0:T(8,128)(2,1)} %param.8) | copy-start | bytes 344068
  192.9 1.2 collective-permute-start.23
  194.1 3.5 %collective-permute-start.24 = (f32[8]{0:T(128)S(1)}, f32[8]{0:T(128)S(1)}, u32[]{:S(2)}, u32[]{:S(2)}) collective-permute-start(f32[8]{0:T(128)S(1)} %add.341), channel_id=1, source_target_pairs={{0,2},{2,0},{1,3},{3,1},{4,6},{6,4},{5,7},{7,5},{8,10},{10,8},{9,1... | collective-permute-start | bytes 104 | tf_op jit(solution)/shard_map/ppermute | solution.py:38
  197.6 3.5 %collective-permute-start.25 = (f32[8]{0:T(128)S(1)}, f32[8]{0:T(128)S(1)}, u32[]{:S(2)}, u32[]{:S(2)}) collective-permute-start(f32[8]{0:T(128)S(1)} %add.342), channel_id=1, source_target_pairs={{0,4},{4,0},{8,12},{12,8},{1,5},{5,1},{9,13},{13,9},{2,6},{6,2},{1... | collective-permute-start | bytes 104 | tf_op jit(solution)/shard_map/ppermute | solution.py:38
  201.2 4.4 %collective-permute-start.26 = (f32[8]{0:T(128)S(1)}, f32[8]{0:T(128)S(1)}, u32[]{:S(2)}, u32[]{:S(2)}) collective-permute-start(f32[8]{0:T(128)S(1)} %add.343), channel_id=1, source_target_pairs={{0,8},{4,12},{8,0},{12,4},{1,9},{5,13},{9,1},{13,5},{2,10},{6,14},... | collective-permute-start | bytes 104 | tf_op jit(solution)/shard_map/ppermute | solution.py:38

commit v5 on v4

--- a/solution.py
+++ b/solution.py
@@ -9,7 +9,7 @@
 FF = 28672
 MEMBERS = 8
 SEQ = 128
-SHARES = (2, 3, 2, 1)
+SHARES = (2, 2, 2, 2)
 SPAN = 250.0
 FLOOR = -124.0
 

time: 222 us -> 198 us (0.89)
  waiting for transfers between devices: 93.1 us -> 71.7 us
  starting transfers between devices: 19.6 us -> 24.7 us
  local copies, waits for them, and re-layouts: 12.9 us -> 8.21 us
  matrix products: 77.5 us -> 74.9 us
    ppermute x27, waiting for transfers between devices: 93.1 us -> 71.7 us  [exchanged(): return lax.ppermute(block, axis, route)]
    ppermute x27, starting transfers between devices: 19.6 us -> 24.7 us  [exchanged(): return lax.ppermute(block, axis, route)]
    dot_general x4, matrix products: 59.7 us -> 57.2 us  [piece_product(): product = jnp.dot(rows, weight, preferred_element_type=jnp.float32)]
  transfers between devices with their start and end apart: 27 -> 27, of which waited for: 12 -> 13; matrix products, arithmetic and copies ran while one was open for 37% -> 39% of each run, Pallas kernels for 0% -> 0%
where the time goes in v5:
time: 198 us
  matrix products  74.9 us (38%)
  waiting for transfers between devices  71.7 us (36%)
  starting transfers between devices  24.7 us (12%)
  other arithmetic  16.5 us (8%)
  local copies, waits for them, and re-layouts  8.21 us (4%)
    ppermute x27, waiting for transfers between devices, exchanged(): return lax.ppermute(block, axis, route)  71.7 us
    dot_general x4, matrix products, piece_product(): product = jnp.dot(rows, weight, preferred_element_type=jnp.float32)  57.2 us
    ppermute x27, starting transfers between devices, exchanged(): return lax.ppermute(block, axis, route)  24.7 us
    dot_general x1, matrix products, per_device(): lax.dot_general(left, right, (((0,), (0,)), ((), ())), preferred_element_...  14.6 us
  transfers between devices with their start and end apart: 27, of which 13 were waited for; matrix products, arithmetic and copies ran while one was open for 39% of the time, Pallas kernels for 0%

profile of v5, /device:TPU:0, one launch (start us, length us, event | category | flops | bytes accessed | tf_op | source)
XLA Modules:
  0.0 197.9 jit_solution(5424222792943515761)
XLA Ops:
  0.6 3.5 %slice_bitcast_fusion.1 = (bf16[64,7168]{1,0:T(8,128)(2,1)}, bf16[64,7168]{1,0:T(8,128)(2,1)}, bf16[64,7168]{1,0:T(8,128)(2,1)S(1)}, bf16[64,7168]{1,0:T(8,128)(2,1)S(1)}) fusion(bf16[1,256,7168]{2,1,0:T(8,128)(2,1)} %bitcast.112), kind=kLoop, calls=%fused_computation.108 | loop fusion | bytes 7340032 | tf_op jit(solution)/shard_map/reshape | solution.py:97
  4.1 2.9 %collective-permute-start.1 = (bf16[64,7168]{1,0:T(8,128)(2,1)S(1)}, bf16[64,7168]{1,0:T(8,128)(2,1)}, u32[]{:S(2)}, u32[]{:S(2)}) collective-permute-start(bf16[64,7168]{1,0:T(8,128)(2,1)S(1)} %get-tuple-element.26), channel_id=1, source_target_pairs={{0,2},{2,0},{1,3},{3,1},{4,6},{6,4},{5,7},{7,5},{8,10},{10,8},{9,1... | collective-permute-start | bytes 2752520 | tf_op jit(solution)/shard_map/ppermute | solution.py:38
  7.1 0.6 gather_fusion
  7.9 3.1 %fusion.103 = f32[8,1,32]{2,1,0:T(1,128)S(1)} fusion(bf16[8,32,7168]{2,1,0:T(8,128)(2,1)} %bitcast.113, bf16[8,7168,1]{1,0,2:T(8,128)(2,1)S(1)} %select_bitcast_fusion), kind=kOutput, calls=%fused_computation.172 | convolution fusion | flops 3670016 | bytes 3785728 | tf_op jit(solution)/shard_map/buhf,buf->buh/dot_general | solution.py:83
  11.0 0.5 collective-permute-start
  11.7 0.7 gather_fusion.1
  12.4 15.1 %collective-permute-done.1 = bf16[64,7168]{1,0:T(8,128)(2,1)} collective-permute-done((bf16[64,7168]{1,0:T(8,128)(2,1)S(1)}, bf16[64,7168]{1,0:T(8,128)(2,1)}, u32[]{:S(2)}, u32[]{:S(2)}) %collective-permute-start.1) | collective-permute-done | bytes 917536 | tf_op jit(solution)/shard_map/ppermute | solution.py:38
  27.9 0.6 collective-permute-start.5
  28.5 1.6 collective-permute-done.5
  30.4 1.7 collective-permute-start.8
  32.2 0.3 collective-permute-start.12
  32.5 0.2 collective-permute-start.11
  32.8 14.1 %fusion = f32[256,2048]{1,0:T(8,128)S(1)} fusion(bf16[7168,2048]{1,0:T(8,128)(2,1)} %param.7, bf16[64,7168]{1,0:T(8,128)(2,1)} %collective-permute-done.2, bf16[64,7168]{1,0:T(8,128)(2,1)} %collective-permute-done.1, bf16[64,7168]{1,0:T(8,128)(2,1)} %collective-permute-done, bf16[64,7168]{1,0:T(8,128)(2,1)S(1)} %get-tuple-element.26), kind=kOutput, calls=%fused_computation.3 | convolution fusion | flops 7530872832 | bytes 35127296 | tf_op jit(solution)/shard_map/dot_general | solution.py:54
  46.9 0.2 mul.402
  47.1 0.3 multiply_add_fusion
  47.6 6.1 %collective-permute-done.8 = bf16[64,7168]{1,0:T(8,128)(2,1)} collective-permute-done((bf16[64,7168]{1,0:T(8,128)(2,1)S(1)}, bf16[64,7168]{1,0:T(8,128)(2,1)}, u32[]{:S(2)}, u32[]{:S(2)}) %collective-permute-start.8) | collective-permute-done | bytes 917536 | tf_op jit(solution)/shard_map/ppermute | solution.py:38
  53.7 0.4 fusion.49
  54.3 1.9 collective-permute-start.6
  56.2 0.2 collective-permute-done.9
  56.4 1.7 collective-permute-start.17
  58.2 13.9 %fusion.8 = f32[256,2048]{1,0:T(8,128)S(1)} fusion(bf16[7168,2048]{1,0:T(8,128)(2,1)} %param.7, bf16[64,7168]{1,0:T(8,128)(2,1)S(1)} %collective-permute-done.9, bf16[64,7168]{1,0:T(8,128)(2,1)} %collective-permute-done.8, bf16[64,7168]{1,0:T(8,128)(2,1)} %collective-permute-done.7, bf16[64,7168]{1,0:T(8,128)(2,1)S(1)} %get-tuple-element.31), kind=kOutput, calls=%fused_computation.11 | convolution fusion | flops 7530872832 | bytes 35127296 | tf_op jit(solution)/shard_map/dot_general | solution.py:54
  72.3 0.3 copy_add_fusion.2
  72.7 0.7 collective-permute-done.12
  73.4 0.4 fusion.50
  73.9 0.9 pad_maximum_fusion.2
  74.7 1.8 collective-permute-start.14
  76.7 15.1 %fusion.16 = f32[256,2048]{1,0:T(8,128)} fusion(bf16[7168,2048]{1,0:T(8,128)(2,1)} %param.7, bf16[64,7168]{1,0:T(8,128)(2,1)S(1)} %collective-permute-done.13, bf16[64,7168]{1,0:T(8,128)(2,1)} %collective-permute-done.12, bf16[64,7168]{1,0:T(8,128)(2,1)} %collective-permute-done.11, bf16[64,7168]{1,0:T(8,128)(2,1)} %get-tuple-element.37), kind=kOutput, calls=%fused_computation.19 | convolution fusion | flops 7530872832 | bytes 35127296 | tf_op jit(solution)/shard_map/dot_general | solution.py:54
  92.0 1.4 copy-done.2
  93.4 0.3 copy_add_fusion.1
  93.8 0.4 fusion.52
  94.3 0.9 pad_maximum_fusion.3
  95.2 1.2 collective-permute-start.19
  96.3 0.9 multiply_reduce_fusion.3
  97.2 1.9 fusion.51
  99.2 0.2 fusion.86
  99.6 2.7 %collective-permute-start.10 = (bf16[1,64,2176]{2,1,0:T(8,128)(2,1)S(1)}, bf16[1,64,2176]{2,1,0:T(8,128)(2,1)S(1)}, u32[]{:S(2)}, u32[]{:S(2)}) collective-permute-start(bf16[1,64,2176]{2,1,0:T(8,128)(2,1)S(1)} %pad_maximum_fusion.5), channel_id=1, source_target_pairs={{0,8},{4,12},{8,0},{12,4},{1,9},{5,13},{9,1},{13,5},{2,10},{6,14},... | collective-permute-start | bytes 835592 | tf_op jit(solution)/shard_map/ppermute | solution.py:38
  102.4 0.2 fusion.89
  102.8 0.4 collective-permute-start.15
  103.2 12.3 %collective-permute-done.10 = bf16[1,64,2176]{2,1,0:T(8,128)(2,1)S(1)} collective-permute-done((bf16[1,64,2176]{2,1,0:T(8,128)(2,1)S(1)}, bf16[1,64,2176]{2,1,0:T(8,128)(2,1)S(1)}, u32[]{:S(2)}, u32[]{:S(2)}) %collective-permute-start.10) | collective-permute-done | bytes 278560 | tf_op jit(solution)/shard_map/ppermute | solution.py:38
  115.7 0.2 fusion.88
  115.9 14.1 %fusion.24 = f32[256,2048]{1,0:T(8,128)S(1)} fusion(bf16[7168,2048]{1,0:T(8,128)(2,1)} %param.7, bf16[64,7168]{1,0:T(8,128)(2,1)S(1)} %collective-permute-done.18, bf16[64,7168]{1,0:T(8,128)(2,1)} %collective-permute-done.17, bf16[64,7168]{1,0:T(8,128)(2,1)} %collective-permute-done.16, bf16[64,7168]{1,0:T(8,128)(2,1)} %get-tuple-element.44), kind=kOutput, calls=%fused_computation.27 | convolution fusion | flops 7530872832 | bytes 35127296 | tf_op jit(solution)/shard_map/dot_general | solution.py:54
  130.1 0.2 mul.444
  130.3 0.3 copy_add_fusion
  130.7 0.4 fusion.54
  131.3 4.0 %collective-permute-start.21 = (bf16[2,64,2176]{2,1,0:T(8,128)(2,1)S(1)}, bf16[2,64,2176]{2,1,0:T(8,128)(2,1)S(1)}, u32[]{:S(2)}, u32[]{:S(2)}) collective-permute-start(bf16[2,64,2176]{2,1,0:T(8,128)(2,1)S(1)} %pad_maximum_fusion.4), channel_id=1, source_target_pairs={{0,4},{4,0},{8,12},{12,8},{1,5},{5,1},{9,13},{13,9},{2,6},{6,2},{1... | collective-permute-start | bytes 1671176 | tf_op jit(solution)/shard_map/ppermute | solution.py:38
  135.4 0.9 multiply_reduce_fusion.2
  136.3 1.5 fusion.55
  137.9 0.2 fusion.92
  138.3 0.2 fusion.91
  138.6 13.4 %collective-permute-done.20 = bf16[1,64,2176]{2,1,0:T(8,128)(2,1)S(1)} collective-permute-done((bf16[1,64,2176]{2,1,0:T(8,128)(2,1)S(1)}, bf16[1,64,2176]{2,1,0:T(8,128)(2,1)S(1)}, u32[]{:S(2)}, u32[]{:S(2)}) %collective-permute-start.20) | collective-permute-done | bytes 278560 | tf_op jit(solution)/shard_map/ppermute | solution.py:38
  152.1 0.6 collective-permute-done.21
  152.8 0.4 fusion.56
  153.4 0.2 fusion.95
  153.7 2.9 %collective-permute-start.22 = (bf16[1,64,2176]{2,1,0:T(8,128)(2,1)S(1)}, bf16[1,64,2176]{2,1,0:T(8,128)(2,1)S(1)}, u32[]{:S(2)}, u32[]{:S(2)}) collective-permute-start(bf16[1,64,2176]{2,1,0:T(8,128)(2,1)S(1)} %pad_maximum_fusion.8), channel_id=1, source_target_pairs={{0,8},{4,12},{8,0},{12,4},{1,9},{5,13},{9,1},{13,5},{2,10},{6,14},... | collective-permute-start | bytes 835592 | tf_op jit(solution)/shard_map/ppermute | solution.py:38
  156.8 10.4 %collective-permute-done.22 = bf16[1,64,2176]{2,1,0:T(8,128)(2,1)S(1)} collective-permute-done((bf16[1,64,2176]{2,1,0:T(8,128)(2,1)S(1)}, bf16[1,64,2176]{2,1,0:T(8,128)(2,1)S(1)}, u32[]{:S(2)}, u32[]{:S(2)}) %collective-permute-start.22) | collective-permute-done | bytes 278560 | tf_op jit(solution)/shard_map/ppermute | solution.py:38
  167.6 1.1 fusion.32
  168.7 0.4 multiply_reduce_fusion
  169.3 1.1 collective-permute-done.23
  170.4 1.5 collective-permute-start.24
  171.9 2.0 %collective-permute-done.24 = f32[8]{0:T(128)S(1)} collective-permute-done((f32[8]{0:T(128)S(1)}, f32[8]{0:T(128)S(1)}, u32[]{:S(2)}, u32[]{:S(2)}) %collective-permute-start.24) | collective-permute-done | bytes 64 | tf_op jit(solution)/shard_map/ppermute | solution.py:38
  173.9 3.5 %collective-permute-done.25 = f32[8]{0:T(128)S(1)} collective-permute-done((f32[8]{0:T(128)S(1)}, f32[8]{0:T(128)S(1)}, u32[]{:S(2)}, u32[]{:S(2)}) %collective-permute-start.25) | collective-permute-done | bytes 64 | tf_op jit(solution)/shard_map/ppermute | solution.py:38
  177.5 4.4 %collective-permute-done.26 = f32[8]{0:T(128)S(1)} collective-permute-done((f32[8]{0:T(128)S(1)}, f32[8]{0:T(128)S(1)}, u32[]{:S(2)}, u32[]{:S(2)}) %collective-permute-start.26) | collective-permute-done | bytes 64 | tf_op jit(solution)/shard_map/ppermute | solution.py:38
  181.9 0.6 fusion.132
  183.3 14.6 %convolution_convert_fusion = bf16[7168,2048]{1,0:T(8,128)(2,1)} fusion(bf16[8,7168]{1,0:T(8,128)(2,1)S(1)} %copy-done.1, bf16[8,2048]{1,0:T(8,128)(2,1)S(1)} %get-tuple-element.59, bf16[8,2048]{1,0:T(8,128)(2,1)S(1)} %get-tuple-element.60, bf16[8,2048]{1,0:T(8,128)(2,1)S(1)} %get-tuple-element.58), kind=kOutput, calls=%fused_computation.2 | convolution fusion | flops 720650240 | bytes 29573120 | tf_op jit(solution)/shard_map/dot_general | solution.py:158
  (101 shorter events, 5.1 us)
Async XLA Ops:
  0.6 6.5 %copy-start.1 = (bf16[8,7168]{1,0:T(8,128)(2,1)S(1)}, bf16[8,7168]{1,0:T(8,128)(2,1)}, u32[]{:S(2)}) copy-start(bf16[8,7168]{1,0:T(8,128)(2,1)} %param.8) | copy-start | bytes 344068
  4.1 23.4 %collective-permute-start.1 = (bf16[64,7168]{1,0:T(8,128)(2,1)S(1)}, bf16[64,7168]{1,0:T(8,128)(2,1)}, u32[]{:S(2)}, u32[]{:S(2)}) collective-permute-start(bf16[64,7168]{1,0:T(8,128)(2,1)S(1)} %get-tuple-element.26), channel_id=1, source_target_pairs={{0,2},{2,0},{1,3},{3,1},{4,6},{6,4},{5,7},{7,5},{8,10},{10,8},{9,1... | collective-permute-start | bytes 2752520 | tf_op jit(solution)/shard_map/ppermute | solution.py:38
  7.9 3.8 %copy-start = (bf16[8,2048]{1,0:T(8,128)(2,1)S(1)}, bf16[8,2048]{1,0:T(8,128)(2,1)}, u32[]{:S(2)}) copy-start(bf16[8,2048]{1,0:T(8,128)(2,1)} %param.9) | copy-start | bytes 98308
  11.0 16.9 %collective-permute-start.4 = (f32[1,8,32]{2,1,0:T(8,128)S(1)}, f32[1,8,32]{2,1,0:T(8,128)S(1)}, u32[]{:S(2)}, u32[]{:S(2)}) collective-permute-start(f32[1,8,32]{2,1,0:T(8,128)S(1)} %bitcast.118), channel_id=1, source_target_pairs={{0,2},{2,0},{1,3},{3,1},{4,6},{6,4},{5,7},{7,5},{8,10},{10,8},{9,1... | collective-permute-start | bytes 3080 | tf_op jit(solution)/shard_map/ppermute | solution.py:38
  11.0 17.5 %collective-permute-start.3 = (f32[1,8,32]{2,1,0:T(8,128)S(1)}, f32[1,8,32]{2,1,0:T(8,128)S(1)}, u32[]{:S(2)}, u32[]{:S(2)}) collective-permute-start(f32[1,8,32]{2,1,0:T(8,128)S(1)} %bitcast.119), channel_id=1, source_target_pairs={{0,1},{1,0},{2,3},{3,2},{4,5},{5,4},{6,7},{7,6},{8,9},{9,8},{10,11... | collective-permute-start | bytes 3080 | tf_op jit(solution)/shard_map/ppermute | solution.py:38
  11.0 21.2 %collective-permute-start = (bf16[64,7168]{1,0:T(8,128)(2,1)S(1)}, bf16[64,7168]{1,0:T(8,128)(2,1)}, u32[]{:S(2)}, u32[]{:S(2)}) collective-permute-start(bf16[64,7168]{1,0:T(8,128)(2,1)S(1)} %get-tuple-element.26), channel_id=1, source_target_pairs={{0,1},{1,0},{2,3},{3,2},{4,5},{5,4},{6,7},{7,6},{8,9},{9,8},{10,11... | collective-permute-start | bytes 2752520 | tf_op jit(solution)/shard_map/ppermute | solution.py:38
  27.6 4.6 %collective-permute-start.2 = (bf16[64,7168]{1,0:T(8,128)(2,1)}, bf16[64,7168]{1,0:T(8,128)(2,1)}, u32[]{:S(2)}, u32[]{:S(2)}) collective-permute-start(bf16[64,7168]{1,0:T(8,128)(2,1)} %collective-permute-done.1), channel_id=1, source_target_pairs={{0,1},{1,0},{2,3},{3,2},{4,5},{5,4},{6,7},{7,6},{8,9},{9,8},{10,11... | collective-permute-start | bytes 2752520 | tf_op jit(solution)/shard_map/ppermute | solution.py:38
  27.9 2.2 %collective-permute-start.5 = (f32[1,8,32]{2,1,0:T(8,128)S(1)}, f32[1,8,32]{2,1,0:T(8,128)S(1)}, u32[]{:S(2)}, u32[]{:S(2)}) collective-permute-start(f32[1,8,32]{2,1,0:T(8,128)S(1)} %collective-permute-done.4), channel_id=1, source_target_pairs={{0,1},{1,0},{2,3},{3,2},{4,5},{5,4},{6,7},{7,6},{8,9},{9,8},{10,11... | collective-permute-start | bytes 3080 | tf_op jit(solution)/shard_map/ppermute | solution.py:38
  30.4 23.3 %collective-permute-start.8 = (bf16[64,7168]{1,0:T(8,128)(2,1)S(1)}, bf16[64,7168]{1,0:T(8,128)(2,1)}, u32[]{:S(2)}, u32[]{:S(2)}) collective-permute-start(bf16[64,7168]{1,0:T(8,128)(2,1)S(1)} %get-tuple-element.31), channel_id=1, source_target_pairs={{0,2},{2,0},{1,3},{3,1},{4,6},{6,4},{5,7},{7,5},{8,10},{10,8},{9,1... | collective-permute-start | bytes 2752520 | tf_op jit(solution)/shard_map/ppermute | solution.py:38
  32.2 24.0 %collective-permute-start.7 = (bf16[64,7168]{1,0:T(8,128)(2,1)S(1)}, bf16[64,7168]{1,0:T(8,128)(2,1)}, u32[]{:S(2)}, u32[]{:S(2)}) collective-permute-start(bf16[64,7168]{1,0:T(8,128)(2,1)S(1)} %get-tuple-element.31), channel_id=1, source_target_pairs={{0,1},{1,0},{2,3},{3,2},{4,5},{5,4},{6,7},{7,6},{8,9},{9,8},{10,11... | collective-permute-start | bytes 2752520 | tf_op jit(solution)/shard_map/ppermute | solution.py:38
  32.2 41.2 %collective-permute-start.12 = (bf16[64,7168]{1,0:T(8,128)(2,1)}, bf16[64,7168]{1,0:T(8,128)(2,1)}, u32[]{:S(2)}, u32[]{:S(2)}) collective-permute-start(bf16[64,7168]{1,0:T(8,128)(2,1)} %get-tuple-element.37), channel_id=1, source_target_pairs={{0,2},{2,0},{1,3},{3,1},{4,6},{6,4},{5,7},{7,5},{8,10},{10,8},{9,1... | collective-permute-start | bytes 2752520 | tf_op jit(solution)/shard_map/ppermute | solution.py:38
  32.5 44.1 %collective-permute-start.11 = (bf16[64,7168]{1,0:T(8,128)(2,1)}, bf16[64,7168]{1,0:T(8,128)(2,1)}, u32[]{:S(2)}, u32[]{:S(2)}) collective-permute-start(bf16[64,7168]{1,0:T(8,128)(2,1)} %get-tuple-element.37), channel_id=1, source_target_pairs={{0,1},{1,0},{2,3},{3,2},{4,5},{5,4},{6,7},{7,6},{8,9},{9,8},{10,11... | collective-permute-start | bytes 2752520 | tf_op jit(solution)/shard_map/ppermute | solution.py:38
  53.7 2.7 %collective-permute-start.9 = (bf16[64,7168]{1,0:T(8,128)(2,1)}, bf16[64,7168]{1,0:T(8,128)(2,1)S(1)}, u32[]{:S(2)}, u32[]{:S(2)}) collective-permute-start(bf16[64,7168]{1,0:T(8,128)(2,1)} %collective-permute-done.8), channel_id=1, source_target_pairs={{0,1},{1,0},{2,3},{3,2},{4,5},{5,4},{6,7},{7,6},{8,9},{9,8},{10,11... | collective-permute-start | bytes 2752520 | tf_op jit(solution)/shard_map/ppermute | solution.py:38
  54.3 20.5 %collective-permute-start.6 = (bf16[2,64,2176]{2,1,0:T(8,128)(2,1)S(1)}, bf16[2,64,2176]{2,1,0:T(8,128)(2,1)S(1)}, u32[]{:S(2)}, u32[]{:S(2)}) collective-permute-start(bf16[2,64,2176]{2,1,0:T(8,128)(2,1)S(1)} %pad_maximum_fusion.1), channel_id=1, source_target_pairs={{0,4},{4,0},{8,12},{12,8},{1,5},{5,1},{9,13},{13,9},{2,6},{6,2},{1... | collective-permute-start | bytes 1671176 | tf_op jit(solution)/shard_map/ppermute | solution.py:38
  56.4 46.2 %collective-permute-start.17 = (bf16[64,7168]{1,0:T(8,128)(2,1)}, bf16[64,7168]{1,0:T(8,128)(2,1)}, u32[]{:S(2)}, u32[]{:S(2)}) collective-permute-start(bf16[64,7168]{1,0:T(8,128)(2,1)} %get-tuple-element.44), channel_id=1, source_target_pairs={{0,2},{2,0},{1,3},{3,1},{4,6},{6,4},{5,7},{7,5},{8,10},{10,8},{9,1... | collective-permute-start | bytes 2752520 | tf_op jit(solution)/shard_map/ppermute | solution.py:38
  58.2 57.7 %collective-permute-start.16 = (bf16[64,7168]{1,0:T(8,128)(2,1)}, bf16[64,7168]{1,0:T(8,128)(2,1)}, u32[]{:S(2)}, u32[]{:S(2)}) collective-permute-start(bf16[64,7168]{1,0:T(8,128)(2,1)} %get-tuple-element.44), channel_id=1, source_target_pairs={{0,1},{1,0},{2,3},{3,2},{4,5},{5,4},{6,7},{7,6},{8,9},{9,8},{10,11... | collective-permute-start | bytes 2752520 | tf_op jit(solution)/shard_map/ppermute | solution.py:38
  73.4 3.3 %collective-permute-start.13 = (bf16[64,7168]{1,0:T(8,128)(2,1)}, bf16[64,7168]{1,0:T(8,128)(2,1)S(1)}, u32[]{:S(2)}, u32[]{:S(2)}) collective-permute-start(bf16[64,7168]{1,0:T(8,128)(2,1)} %collective-permute-done.12), channel_id=1, source_target_pairs={{0,1},{1,0},{2,3},{3,2},{4,5},{5,4},{6,7},{7,6},{8,9},{9,8},{10,11... | collective-permute-start | bytes 2752520 | tf_op jit(solution)/shard_map/ppermute | solution.py:38
  74.7 21.6 %collective-permute-start.14 = (bf16[2,64,2176]{2,1,0:T(8,128)(2,1)}, bf16[2,64,2176]{2,1,0:T(8,128)(2,1)}, u32[]{:S(2)}, u32[]{:S(2)}) collective-permute-start(bf16[2,64,2176]{2,1,0:T(8,128)(2,1)} %pad_maximum_fusion.2), channel_id=1, source_target_pairs={{0,4},{4,0},{8,12},{12,8},{1,5},{5,1},{9,13},{13,9},{2,6},{6,2},{1... | collective-permute-start | bytes 1671176 | tf_op jit(solution)/shard_map/ppermute | solution.py:38
  91.8 1.6 copy-start.2
  95.2 40.2 %collective-permute-start.19 = (bf16[2,64,2176]{2,1,0:T(8,128)(2,1)}, bf16[2,64,2176]{2,1,0:T(8,128)(2,1)}, u32[]{:S(2)}, u32[]{:S(2)}) collective-permute-start(bf16[2,64,2176]{2,1,0:T(8,128)(2,1)} %pad_maximum_fusion.3), channel_id=1, source_target_pairs={{0,4},{4,0},{8,12},{12,8},{1,5},{5,1},{9,13},{13,9},{2,6},{6,2},{1... | collective-permute-start | bytes 1671176 | tf_op jit(solution)/shard_map/ppermute | solution.py:38
  99.6 16.0 %collective-permute-start.10 = (bf16[1,64,2176]{2,1,0:T(8,128)(2,1)S(1)}, bf16[1,64,2176]{2,1,0:T(8,128)(2,1)S(1)}, u32[]{:S(2)}, u32[]{:S(2)}) collective-permute-start(bf16[1,64,2176]{2,1,0:T(8,128)(2,1)S(1)} %pad_maximum_fusion.5), channel_id=1, source_target_pairs={{0,8},{4,12},{8,0},{12,4},{1,9},{5,13},{9,1},{13,5},{2,10},{6,14},... | collective-permute-start | bytes 835592 | tf_op jit(solution)/shard_map/ppermute | solution.py:38
  102.6 13.3 %collective-permute-start.18 = (bf16[64,7168]{1,0:T(8,128)(2,1)}, bf16[64,7168]{1,0:T(8,128)(2,1)S(1)}, u32[]{:S(2)}, u32[]{:S(2)}) collective-permute-start(bf16[64,7168]{1,0:T(8,128)(2,1)} %collective-permute-done.17), channel_id=1, source_target_pairs={{0,1},{1,0},{2,3},{3,2},{4,5},{5,4},{6,7},{7,6},{8,9},{9,8},{10,11... | collective-permute-start | bytes 2752520 | tf_op jit(solution)/shard_map/ppermute | solution.py:38
  102.8 32.5 %collective-permute-start.15 = (bf16[1,64,2176]{2,1,0:T(8,128)(2,1)S(1)}, bf16[1,64,2176]{2,1,0:T(8,128)(2,1)S(1)}, u32[]{:S(2)}, u32[]{:S(2)}) collective-permute-start(bf16[1,64,2176]{2,1,0:T(8,128)(2,1)S(1)} %pad_maximum_fusion.6), channel_id=1, source_target_pairs={{0,8},{4,12},{8,0},{12,4},{1,9},{5,13},{9,1},{13,5},{2,10},{6,14},... | collective-permute-start | bytes 835592 | tf_op jit(solution)/shard_map/ppermute | solution.py:38
  131.3 21.4 %collective-permute-start.21 = (bf16[2,64,2176]{2,1,0:T(8,128)(2,1)S(1)}, bf16[2,64,2176]{2,1,0:T(8,128)(2,1)S(1)}, u32[]{:S(2)}, u32[]{:S(2)}) collective-permute-start(bf16[2,64,2176]{2,1,0:T(8,128)(2,1)S(1)} %pad_maximum_fusion.4), channel_id=1, source_target_pairs={{0,4},{4,0},{8,12},{12,8},{1,5},{5,1},{9,13},{13,9},{2,6},{6,2},{1... | collective-permute-start | bytes 1671176 | tf_op jit(solution)/shard_map/ppermute | solution.py:38
  138.2 13.7 %collective-permute-start.20 = (bf16[1,64,2176]{2,1,0:T(8,128)(2,1)S(1)}, bf16[1,64,2176]{2,1,0:T(8,128)(2,1)S(1)}, u32[]{:S(2)}, u32[]{:S(2)}) collective-permute-start(bf16[1,64,2176]{2,1,0:T(8,128)(2,1)S(1)} %pad_maximum_fusion.7), channel_id=1, source_target_pairs={{0,8},{4,12},{8,0},{12,4},{1,9},{5,13},{9,1},{13,5},{2,10},{6,14},... | collective-permute-start | bytes 835592 | tf_op jit(solution)/shard_map/ppermute | solution.py:38
  153.7 13.5 %collective-permute-start.22 = (bf16[1,64,2176]{2,1,0:T(8,128)(2,1)S(1)}, bf16[1,64,2176]{2,1,0:T(8,128)(2,1)S(1)}, u32[]{:S(2)}, u32[]{:S(2)}) collective-permute-start(bf16[1,64,2176]{2,1,0:T(8,128)(2,1)S(1)} %pad_maximum_fusion.8), channel_id=1, source_target_pairs={{0,8},{4,12},{8,0},{12,4},{1,9},{5,13},{9,1},{13,5},{2,10},{6,14},... | collective-permute-start | bytes 835592 | tf_op jit(solution)/shard_map/ppermute | solution.py:38
  167.3 1.4 copy-start.3
  169.2 1.2 collective-permute-start.23
  170.4 3.5 %collective-permute-start.24 = (f32[8]{0:T(128)S(1)}, f32[8]{0:T(128)S(1)}, u32[]{:S(2)}, u32[]{:S(2)}) collective-permute-start(f32[8]{0:T(128)S(1)} %add.335), channel_id=1, source_target_pairs={{0,2},{2,0},{1,3},{3,1},{4,6},{6,4},{5,7},{7,5},{8,10},{10,8},{9,1... | collective-permute-start | bytes 104 | tf_op jit(solution)/shard_map/ppermute | solution.py:38
  173.9 3.5 %collective-permute-start.25 = (f32[8]{0:T(128)S(1)}, f32[8]{0:T(128)S(1)}, u32[]{:S(2)}, u32[]{:S(2)}) collective-permute-start(f32[8]{0:T(128)S(1)} %add.336), channel_id=1, source_target_pairs={{0,4},{4,0},{8,12},{12,8},{1,5},{5,1},{9,13},{13,9},{2,6},{6,2},{1... | collective-permute-start | bytes 104 | tf_op jit(solution)/shard_map/ppermute | solution.py:38
  177.5 4.4 %collective-permute-start.26 = (f32[8]{0:T(128)S(1)}, f32[8]{0:T(128)S(1)}, u32[]{:S(2)}, u32[]{:S(2)}) collective-permute-start(f32[8]{0:T(128)S(1)} %add.337), channel_id=1, source_target_pairs={{0,8},{4,12},{8,0},{12,4},{1,9},{5,13},{9,1},{13,5},{2,10},{6,14},... | collective-permute-start | bytes 104 | tf_op jit(solution)/shard_map/ppermute | solution.py:38
